TPU v7x, 512 devices: a whole 4x4x16 slice. The times are simulated.
512 devices in a mesh: gx: 8 (over y, core), gy: 64 (over x, z).
Axes of the slice: x: 4, y: 4, z: 16, core: 2. Of those that a mesh axis runs over, the one named last changes fastest.
Arguments:
- coords: bfloat16 [3, 2097152], P(None, ('gx', 'gy')), may hold values from -6 to 6
- vectors: float32 [16, 2097152], P(None, ('gx', 'gy')), may hold values from -6 to 6
- basis: bfloat16 [4096, 512, 128], P(('gx', 'gy')), may hold values from -0.25 to 0.25
- leaf_up: bfloat16 [4096, 128, 128], P(('gx', 'gy')), may hold values from -0.1875 to 0.1875
- mid_up: bfloat16 [512, 128, 128], P(('gx', 'gy')), may hold values from -0.1875 to 0.1875
- top_up: bfloat16 [64, 128, 128], P('gx'), may hold values from -0.1875 to 0.1875
- couple_one: bfloat16 [512, 6, 128, 128], P(('gx', 'gy')), may hold values from -0.21875 to 0.21875
- couple_two: bfloat16 [64, 6, 128, 128], P('gx'), may hold values from -0.21875 to 0.21875
- couple_three: bfloat16 [8, 6, 128, 128], P('gx'), may hold values from -0.21875 to 0.21875
- far_one: int32 [512, 6], P(('gx', 'gy')), may hold values from 0 to 63
- far_two: int32 [64, 6], P('gx'), may hold values from 0 to 7
- far_three: int32 [8, 6], P('gx'), may hold values from 0 to 7
- near_list: int32 [4096, 16], P(('gx', 'gy')), may hold values from 0 to 23
- near_count: int32 [4096], P(('gx', 'gy')), may hold values from 1 to 16, as said below
Outputs:
- product: float32 [16, 2097152], P(None, ('gx', 'gy'))
Inputs may be any that keep to these rules, and one draw needn't show every extreme that they name: `near_count`: each leaf box has 1 to 16 live near slots; some box has 16 in every draw; loads differ from device to device.
All inputs are finite; a program needn't handle non-finite values.
Results may differ from a plain program's by a relative error of at most 0.007.
Values may be sent and summed in bfloat16 or wider, within the bound.
A program may use at most 64 MiB of HBM per device.

v0:
```python
import jax
import jax.numpy as jnp
from jax import lax
from jax.sharding import PartitionSpec as P

NEAR = 16


def extended(cells, sides, width):
    for axis, dim in sides:
        count = lax.axis_size(axis)
        ends = count - 1
        head = lax.slice_in_dim(cells, 0, width, axis=dim)
        tail = lax.slice_in_dim(cells, cells.shape[dim] - width, cells.shape[dim], axis=dim)
        cells = jnp.concatenate(
            [
                lax.ppermute(tail, axis, [(i, (i + 1) % count) for i in range(ends)]),
                cells,
                lax.ppermute(head, axis, [((i + 1) % count, i) for i in range(ends)]),
            ],
            axis=dim,
        )
    return cells


def kernel_tile(targets, sources):
    dist_sq = jnp.zeros((targets.shape[1], targets.shape[2], sources.shape[2]), jnp.float32)
    for comp in range(3):
        delta = targets[comp][:, :, None] - sources[comp][:, None, :]
        dist_sq = dist_sq + delta * delta
    return jnp.exp(-jnp.sqrt(dist_sq)).astype(jnp.bfloat16)


def near_field(window, targets, near_list, near_count, stop):
    boxes = targets.shape[1]
    points = targets.shape[2]
    probes = window.shape[0] - 3
    probe_bf = window[3:]
    places = window[:3].astype(jnp.float32)

    def slot(step, total):
        index = lax.dynamic_index_in_dim(near_list, step, 1, keepdims=False)
        live = step < near_count
        sources = jnp.take(places, index, axis=1)
        tile = kernel_tile(targets, sources)
        picked = jnp.take(probe_bf, index, axis=1)
        values = jnp.where(live[None, :, None], picked, jnp.zeros_like(picked))
        return total + jnp.einsum("bts,qbs->qbt", tile, values, preferred_element_type=jnp.float32)

    empty = jnp.zeros((probes, boxes, points), jnp.float32)
    return lax.fori_loop(0, stop, slot, empty)


def local(
    coords,
    vectors,
    basis,
    leaf_up,
    mid_up,
    top_up,
    couple_one,
    couple_two,
    couple_three,
    far_one,
    far_two,
    far_three,
    near_list,
    near_count,
):
    boxes = basis.shape[0]
    points = basis.shape[1]
    rank = basis.shape[2]
    probes = vectors.shape[0]
    groups = top_up.shape[0]
    bf = jnp.bfloat16
    vec_round = vectors.astype(bf)
    packed = jnp.concatenate([coords, vec_round], axis=0)
    window = extended(packed, (("gy", 1),), boxes * points)
    window = window.reshape(3 + probes, 3 * boxes, points)
    targets = coords.astype(jnp.float32).reshape(3, boxes, points)
    stop = NEAR
    near_part = near_field(window, targets, near_list, near_count, stop)
    vec_boxes = vec_round.reshape(probes, boxes, points)
    leaf_coef = jnp.einsum("qbp,bpr->bqr", vec_boxes, basis, preferred_element_type=jnp.float32)
    level_one = jnp.einsum(
        "bqr,brs->qs", leaf_coef.astype(bf), leaf_up, preferred_element_type=jnp.float32
    )
    one_round = level_one.astype(bf)
    toward_two = jnp.dot(one_round, mid_up[0], preferred_element_type=jnp.float32)
    group = lax.axis_index("gy") // 8
    row_one = lax.all_gather(one_round[None], "gy", axis=0, tiled=True)
    row_two = lax.all_gather(toward_two[None], "gy", axis=0, tiled=True)
    level_two = row_two.reshape(groups, 8, probes, rank).sum(axis=1)
    level_three = jnp.einsum(
        "jqr,jrs->qs", level_two.astype(bf), top_up, preferred_element_type=jnp.float32
    )
    all_three = lax.all_gather(level_three.astype(bf)[None], "gx", axis=0, tiled=True)
    src_three = jnp.take(all_three, far_three[0], axis=0)
    local_three = jnp.einsum(
        "fqr,frs->qs", src_three, couple_three[0], preferred_element_type=jnp.float32
    )
    list_two = lax.dynamic_index_in_dim(far_two, group, 0, keepdims=False)
    pairs_two = lax.dynamic_index_in_dim(couple_two, group, 0, keepdims=False)
    top_mine = lax.dynamic_index_in_dim(top_up, group, 0, keepdims=False)
    src_two = jnp.take(level_two, list_two, axis=0)
    local_two = jnp.einsum(
        "fqr,frs->qs", src_two.astype(bf), pairs_two, preferred_element_type=jnp.float32
    )
    local_two = local_two + jnp.einsum(
        "qs,rs->qr", local_three.astype(bf), top_mine, preferred_element_type=jnp.float32
    )
    src_one = jnp.take(row_one, far_one[0], axis=0)
    local_one = jnp.einsum(
        "fqr,frs->qs", src_one, couple_one[0], preferred_element_type=jnp.float32
    )
    local_one = local_one + jnp.einsum(
        "qs,rs->qr", local_two.astype(bf), mid_up[0], preferred_element_type=jnp.float32
    )
    local_leaf = jnp.einsum(
        "qs,brs->bqr", local_one.astype(bf), leaf_up, preferred_element_type=jnp.float32
    )
    far_part = jnp.einsum(
        "bqr,bpr->qbp", local_leaf.astype(bf), basis, preferred_element_type=jnp.float32
    )
    total = near_part * points ** (-0.5) + far_part
    return total.reshape(probes, boxes * points)


def solution(mesh):
    return jax.shard_map(
        local,
        mesh=mesh,
        in_specs=(
            P(None, ("gx", "gy")),
            P(None, ("gx", "gy")),
            P(("gx", "gy"), None, None),
            P(("gx", "gy"), None, None),
            P(("gx", "gy"), None, None),
            P("gx", None, None),
            P(("gx", "gy"), None, None, None),
            P("gx", None, None, None),
            P("gx", None, None, None),
            P(("gx", "gy"), None),
            P("gx", None),
            P("gx", None),
            P(("gx", "gy"), None),
            P(("gx", "gy")),
        ),
        out_specs=P(None, ("gx", "gy")),
        check_vma=False,
    )
```

profile of v0, /device:TPU:6, one launch (start us, length us, event | category | flops | bytes accessed | tf_op | source)
XLA Modules:
  0.0 405.2 jit_solution(11701002145939565109)
XLA Ops:
  1.1 1.5 pad_maximum_fusion.1
  2.7 11.7 %collective-permute-start.1 = (bf16[19,4096]{1,0:T(8,128)(2,1)}, bf16[19,4096]{1,0:T(8,128)(2,1)S(1)}, u32[]{:S(2)}, u32[]{:S(2)}) collective-permute-start(bf16[19,4096]{1,0:T(8,128)(2,1)} %pad_maximum_fusion.1), channel_id=1, source_target_pairs={{1,0},{2,1},{3,2},{4,3},{5,4},{6,5},{7,6},{8,7},{9,8},{10,9},{11,1... | collective-permute-start | bytes 466952 | tf_op jit(solution)/shard_map/ppermute | solution.py:19
  14.3 1.9 collective-permute-start
  19.7 1.7 fusion.21
  21.4 81.5 %all-gather = bf16[1024,128]{1,0:T(8,128)(2,1)S(1)} all-gather(bf16[16,128]{1,0:T(8,128)(2,1)S(1)} %fusion.21), channel_id=2, replica_groups=mesh['gx'=8,'gy'=64] {'gy'}, dimensions={0}, use_global_device_ids=true | all-gather | bytes 266240 | tf_op jit(solution)/shard_map/all_gather | solution.py:91
  103.0 98.3 %all-gather.1 = f32[1024,128]{1,0:T(8,128)S(1)} all-gather(f32[16,128]{1,0:T(8,128)S(1)} %fusion.34), channel_id=3, replica_groups=mesh['gx'=8,'gy'=64] {'gy'}, dimensions={0}, use_global_device_ids=true | all-gather | bytes 532480 | tf_op jit(solution)/shard_map/all_gather | solution.py:92
  202.1 13.3 %all-gather.2 = bf16[128,128]{1,0:T(8,128)(2,1)S(1)} all-gather(bf16[16,128]{1,0:T(8,128)(2,1)S(1)} %fusion.17), channel_id=4, replica_groups=mesh['gx'=8,'gy'=64] {'gx'}, dimensions={0}, use_global_device_ids=true | all-gather | bytes 36864 | tf_op jit(solution)/shard_map/all_gather | solution.py:97
  220.6 182.4 %while.14 = (s32[]{:T(128)}, f32[16,8,512]{2,0,1:T(8,128)}, s32[8]{0:T(128)}, s32[8,16]{0,1:T(8,128)}, bf16[16,24,512]{2,0,1:T(8,128)(2,1)S(1)}, /*index=5*/f32[...) while((s32[]{:T(128)}, f32[16,8,512]{2,0,1:T(8,128)}, s32[8]{0:T(128)}, ...), condition=%wide.region_1.2_spmd.clone, body=%wide.region_0.1_spmd.clone.sunk | while | flops 88355896 | bytes 1528247 | solution.py:51
  222.7 1.5 gather_fusion
  225.1 6.9 %fusion.73 = f32[16,8,512]{2,0,1:T(8,128)} fusion(f32[8,512]{1,0:T(8,128)S(1)} %get-tuple-element.260, f32[8,512]{1,0:T(8,128)S(1)} %get-tuple-element.262, f32[8,512]{1,0:T(8,128)S(1)} %get-tuple-element.263, f32[8,512]{1,0:T(8,128)S(1)} %get-tuple-element.264, f32[8,512]{1,0:T(8,128)S(1)} %get-tuple-element.265, ...), kind=kOutput, calls=%fused_computation.8.clone.1 | convolution fusion | flops 88342528 | bytes 753681 | tf_op jit(solution)/shard_map/while/body/eval_jaxpr/bts,qbs->qbt/dot_general | solution.py:48
  236.3 7.1 %fusion.73 = f32[16,8,512]{2,0,1:T(8,128)} fusion(f32[8,512]{1,0:T(8,128)S(1)} %get-tuple-element.260, f32[8,512]{1,0:T(8,128)S(1)} %get-tuple-element.262, f32[8,512]{1,0:T(8,128)S(1)} %get-tuple-element.263, f32[8,512]{1,0:T(8,128)S(1)} %get-tuple-element.264, f32[8,512]{1,0:T(8,128)S(1)} %get-tuple-element.265, ...), kind=kOutput, calls=%fused_computation.8.clone.1 | convolution fusion | flops 88342528 | bytes 753681 | tf_op jit(solution)/shard_map/while/body/eval_jaxpr/bts,qbs->qbt/dot_general | solution.py:48
  245.3 1.5 gather_fusion
  247.7 7.1 %fusion.73 = f32[16,8,512]{2,0,1:T(8,128)} fusion(f32[8,512]{1,0:T(8,128)S(1)} %get-tuple-element.260, f32[8,512]{1,0:T(8,128)S(1)} %get-tuple-element.262, f32[8,512]{1,0:T(8,128)S(1)} %get-tuple-element.263, f32[8,512]{1,0:T(8,128)S(1)} %get-tuple-element.264, f32[8,512]{1,0:T(8,128)S(1)} %get-tuple-element.265, ...), kind=kOutput, calls=%fused_computation.8.clone.1 | convolution fusion | flops 88342528 | bytes 753681 | tf_op jit(solution)/shard_map/while/body/eval_jaxpr/bts,qbs->qbt/dot_general | solution.py:48
  256.7 1.5 gather_fusion
  259.1 7.1 %fusion.73 = f32[16,8,512]{2,0,1:T(8,128)} fusion(f32[8,512]{1,0:T(8,128)S(1)} %get-tuple-element.260, f32[8,512]{1,0:T(8,128)S(1)} %get-tuple-element.262, f32[8,512]{1,0:T(8,128)S(1)} %get-tuple-element.263, f32[8,512]{1,0:T(8,128)S(1)} %get-tuple-element.264, f32[8,512]{1,0:T(8,128)S(1)} %get-tuple-element.265, ...), kind=kOutput, calls=%fused_computation.8.clone.1 | convolution fusion | flops 88342528 | bytes 753681 | tf_op jit(solution)/shard_map/while/body/eval_jaxpr/bts,qbs->qbt/dot_general | solution.py:48
  268.2 1.5 gather_fusion
  270.5 7.1 %fusion.73 = f32[16,8,512]{2,0,1:T(8,128)} fusion(f32[8,512]{1,0:T(8,128)S(1)} %get-tuple-element.260, f32[8,512]{1,0:T(8,128)S(1)} %get-tuple-element.262, f32[8,512]{1,0:T(8,128)S(1)} %get-tuple-element.263, f32[8,512]{1,0:T(8,128)S(1)} %get-tuple-element.264, f32[8,512]{1,0:T(8,128)S(1)} %get-tuple-element.265, ...), kind=kOutput, calls=%fused_computation.8.clone.1 | convolution fusion | flops 88342528 | bytes 753681 | tf_op jit(solution)/shard_map/while/body/eval_jaxpr/bts,qbs->qbt/dot_general | solution.py:48
  279.6 1.5 gather_fusion
  281.9 7.1 %fusion.73 = f32[16,8,512]{2,0,1:T(8,128)} fusion(f32[8,512]{1,0:T(8,128)S(1)} %get-tuple-element.260, f32[8,512]{1,0:T(8,128)S(1)} %get-tuple-element.262, f32[8,512]{1,0:T(8,128)S(1)} %get-tuple-element.263, f32[8,512]{1,0:T(8,128)S(1)} %get-tuple-element.264, f32[8,512]{1,0:T(8,128)S(1)} %get-tuple-element.265, ...), kind=kOutput, calls=%fused_computation.8.clone.1 | convolution fusion | flops 88342528 | bytes 753681 | tf_op jit(solution)/shard_map/while/body/eval_jaxpr/bts,qbs->qbt/dot_general | solution.py:48
  291.0 1.5 gather_fusion
  293.3 7.1 %fusion.73 = f32[16,8,512]{2,0,1:T(8,128)} fusion(f32[8,512]{1,0:T(8,128)S(1)} %get-tuple-element.260, f32[8,512]{1,0:T(8,128)S(1)} %get-tuple-element.262, f32[8,512]{1,0:T(8,128)S(1)} %get-tuple-element.263, f32[8,512]{1,0:T(8,128)S(1)} %get-tuple-element.264, f32[8,512]{1,0:T(8,128)S(1)} %get-tuple-element.265, ...), kind=kOutput, calls=%fused_computation.8.clone.1 | convolution fusion | flops 88342528 | bytes 753681 | tf_op jit(solution)/shard_map/while/body/eval_jaxpr/bts,qbs->qbt/dot_general | solution.py:48
  302.4 1.5 gather_fusion
  304.7 7.1 %fusion.73 = f32[16,8,512]{2,0,1:T(8,128)} fusion(f32[8,512]{1,0:T(8,128)S(1)} %get-tuple-element.260, f32[8,512]{1,0:T(8,128)S(1)} %get-tuple-element.262, f32[8,512]{1,0:T(8,128)S(1)} %get-tuple-element.263, f32[8,512]{1,0:T(8,128)S(1)} %get-tuple-element.264, f32[8,512]{1,0:T(8,128)S(1)} %get-tuple-element.265, ...), kind=kOutput, calls=%fused_computation.8.clone.1 | convolution fusion | flops 88342528 | bytes 753681 | tf_op jit(solution)/shard_map/while/body/eval_jaxpr/bts,qbs->qbt/dot_general | solution.py:48
  313.8 1.5 gather_fusion
  316.1 7.1 %fusion.73 = f32[16,8,512]{2,0,1:T(8,128)} fusion(f32[8,512]{1,0:T(8,128)S(1)} %get-tuple-element.260, f32[8,512]{1,0:T(8,128)S(1)} %get-tuple-element.262, f32[8,512]{1,0:T(8,128)S(1)} %get-tuple-element.263, f32[8,512]{1,0:T(8,128)S(1)} %get-tuple-element.264, f32[8,512]{1,0:T(8,128)S(1)} %get-tuple-element.265, ...), kind=kOutput, calls=%fused_computation.8.clone.1 | convolution fusion | flops 88342528 | bytes 753681 | tf_op jit(solution)/shard_map/while/body/eval_jaxpr/bts,qbs->qbt/dot_general | solution.py:48
  327.6 7.1 %fusion.73 = f32[16,8,512]{2,0,1:T(8,128)} fusion(f32[8,512]{1,0:T(8,128)S(1)} %get-tuple-element.260, f32[8,512]{1,0:T(8,128)S(1)} %get-tuple-element.262, f32[8,512]{1,0:T(8,128)S(1)} %get-tuple-element.263, f32[8,512]{1,0:T(8,128)S(1)} %get-tuple-element.264, f32[8,512]{1,0:T(8,128)S(1)} %get-tuple-element.265, ...), kind=kOutput, calls=%fused_computation.8.clone.1 | convolution fusion | flops 88342528 | bytes 753681 | tf_op jit(solution)/shard_map/while/body/eval_jaxpr/bts,qbs->qbt/dot_general | solution.py:48
  339.0 7.1 %fusion.73 = f32[16,8,512]{2,0,1:T(8,128)} fusion(f32[8,512]{1,0:T(8,128)S(1)} %get-tuple-element.260, f32[8,512]{1,0:T(8,128)S(1)} %get-tuple-element.262, f32[8,512]{1,0:T(8,128)S(1)} %get-tuple-element.263, f32[8,512]{1,0:T(8,128)S(1)} %get-tuple-element.264, f32[8,512]{1,0:T(8,128)S(1)} %get-tuple-element.265, ...), kind=kOutput, calls=%fused_computation.8.clone.1 | convolution fusion | flops 88342528 | bytes 753681 | tf_op jit(solution)/shard_map/while/body/eval_jaxpr/bts,qbs->qbt/dot_general | solution.py:48
  350.4 7.1 %fusion.73 = f32[16,8,512]{2,0,1:T(8,128)} fusion(f32[8,512]{1,0:T(8,128)S(1)} %get-tuple-element.260, f32[8,512]{1,0:T(8,128)S(1)} %get-tuple-element.262, f32[8,512]{1,0:T(8,128)S(1)} %get-tuple-element.263, f32[8,512]{1,0:T(8,128)S(1)} %get-tuple-element.264, f32[8,512]{1,0:T(8,128)S(1)} %get-tuple-element.265, ...), kind=kOutput, calls=%fused_computation.8.clone.1 | convolution fusion | flops 88342528 | bytes 753681 | tf_op jit(solution)/shard_map/while/body/eval_jaxpr/bts,qbs->qbt/dot_general | solution.py:48
  361.8 7.1 %fusion.73 = f32[16,8,512]{2,0,1:T(8,128)} fusion(f32[8,512]{1,0:T(8,128)S(1)} %get-tuple-element.260, f32[8,512]{1,0:T(8,128)S(1)} %get-tuple-element.262, f32[8,512]{1,0:T(8,128)S(1)} %get-tuple-element.263, f32[8,512]{1,0:T(8,128)S(1)} %get-tuple-element.264, f32[8,512]{1,0:T(8,128)S(1)} %get-tuple-element.265, ...), kind=kOutput, calls=%fused_computation.8.clone.1 | convolution fusion | flops 88342528 | bytes 753681 | tf_op jit(solution)/shard_map/while/body/eval_jaxpr/bts,qbs->qbt/dot_general | solution.py:48
  373.2 7.1 %fusion.73 = f32[16,8,512]{2,0,1:T(8,128)} fusion(f32[8,512]{1,0:T(8,128)S(1)} %get-tuple-element.260, f32[8,512]{1,0:T(8,128)S(1)} %get-tuple-element.262, f32[8,512]{1,0:T(8,128)S(1)} %get-tuple-element.263, f32[8,512]{1,0:T(8,128)S(1)} %get-tuple-element.264, f32[8,512]{1,0:T(8,128)S(1)} %get-tuple-element.265, ...), kind=kOutput, calls=%fused_computation.8.clone.1 | convolution fusion | flops 88342528 | bytes 753681 | tf_op jit(solution)/shard_map/while/body/eval_jaxpr/bts,qbs->qbt/dot_general | solution.py:48
  384.6 7.1 %fusion.73 = f32[16,8,512]{2,0,1:T(8,128)} fusion(f32[8,512]{1,0:T(8,128)S(1)} %get-tuple-element.260, f32[8,512]{1,0:T(8,128)S(1)} %get-tuple-element.262, f32[8,512]{1,0:T(8,128)S(1)} %get-tuple-element.263, f32[8,512]{1,0:T(8,128)S(1)} %get-tuple-element.264, f32[8,512]{1,0:T(8,128)S(1)} %get-tuple-element.265, ...), kind=kOutput, calls=%fused_computation.8.clone.1 | convolution fusion | flops 88342528 | bytes 753681 | tf_op jit(solution)/shard_map/while/body/eval_jaxpr/bts,qbs->qbt/dot_general | solution.py:48
  396.0 7.1 %fusion.73 = f32[16,8,512]{2,0,1:T(8,128)} fusion(f32[8,512]{1,0:T(8,128)S(1)} %get-tuple-element.260, f32[8,512]{1,0:T(8,128)S(1)} %get-tuple-element.262, f32[8,512]{1,0:T(8,128)S(1)} %get-tuple-element.263, f32[8,512]{1,0:T(8,128)S(1)} %get-tuple-element.264, f32[8,512]{1,0:T(8,128)S(1)} %get-tuple-element.265, ...), kind=kOutput, calls=%fused_computation.8.clone.1 | convolution fusion | flops 88342528 | bytes 753681 | tf_op jit(solution)/shard_map/while/body/eval_jaxpr/bts,qbs->qbt/dot_general | solution.py:48
  (247 shorter events, 69.0 us)
Async XLA Ops:
  0.0 216.5 %copy-start = (bf16[8,6,128,128]{3,2,1,0:T(8,128)(2,1)S(1)}, bf16[8,6,128,128]{3,2,1,0:T(8,128)(2,1)}, u32[]{:S(2)}) copy-start(bf16[8,6,128,128]{3,2,1,0:T(8,128)(2,1)} %param.23) | copy-start | bytes 4718596
  0.0 102.8 %copy-start.7 = (bf16[1,128,128]{2,1,0:T(8,128)(2,1)S(1)}, bf16[1,128,128]{2,1,0:T(8,128)(2,1)}, u32[]{:S(2)}) copy-start(bf16[1,128,128]{2,1,0:T(8,128)(2,1)} %param.20) | copy-start | bytes 98308
  1.1 200.2 %copy-start.4 = (bf16[8,128,128]{2,1,0:T(8,128)(2,1)S(1)}, bf16[8,128,128]{2,1,0:T(8,128)(2,1)}, u32[]{:S(2)}) copy-start(bf16[8,128,128]{2,1,0:T(8,128)(2,1)} %param.21) | copy-start | bytes 786436
  2.7 217.0 %collective-permute-start.1 = (bf16[19,4096]{1,0:T(8,128)(2,1)}, bf16[19,4096]{1,0:T(8,128)(2,1)S(1)}, u32[]{:S(2)}, u32[]{:S(2)}) collective-permute-start(bf16[19,4096]{1,0:T(8,128)(2,1)} %pad_maximum_fusion.1), channel_id=1, source_target_pairs={{1,0},{2,1},{3,2},{4,3},{5,4},{6,5},{7,6},{8,7},{9,8},{10,9},{11,1... | collective-permute-start | bytes 466952 | tf_op jit(solution)/shard_map/ppermute | solution.py:19
  14.3 205.3 %collective-permute-start = (bf16[19,4096]{1,0:T(8,128)(2,1)}, bf16[19,4096]{1,0:T(8,128)(2,1)S(1)}, u32[]{:S(2)}, u32[]{:S(2)}) collective-permute-start(bf16[19,4096]{1,0:T(8,128)(2,1)} %pad_maximum_fusion.1), channel_id=1, source_target_pairs={{0,1},{1,2},{2,3},{3,4},{4,5},{5,6},{6,7},{7,8},{8,9},{9,10},{10,1... | collective-permute-start | bytes 466952 | tf_op jit(solution)/shard_map/ppermute | solution.py:17
  19.7 198.3 %copy-start.5 = (bf16[1,6,128,128]{3,2,1,0:T(8,128)(2,1)S(1)}, bf16[1,6,128,128]{3,2,1,0:T(8,128)(2,1)}, u32[]{:S(2)}) copy-start(bf16[1,6,128,128]{3,2,1,0:T(8,128)(2,1)} %param.22) | copy-start | bytes 589828
  21.4 196.9 %copy-start.9 = (s32[8,16]{1,0:T(8,128)S(1)}, s32[8,16]{1,0:T(8,128)}, u32[]{:S(2)}) copy-start(s32[8,16]{1,0:T(8,128)} %param.28) | copy-start | bytes 1540
  21.4 197.5 %copy-start.3 = (bf16[3,4096]{1,0:T(4,128)(2,1)S(1)}, bf16[3,4096]{1,0:T(4,128)(2,1)}, u32[]{:S(2)}) copy-start(bf16[3,4096]{1,0:T(4,128)(2,1)} %param.16) | copy-start | bytes 73732
  220.6 182.4 %copy-start.1 = (bf16[8,512,128]{2,1,0:T(8,128)(2,1)S(1)}, bf16[8,512,128]{2,1,0:T(8,128)(2,1)}, u32[]{:S(2)}) copy-start(bf16[8,512,128]{2,1,0:T(8,128)(2,1)} %param.18) | copy-start | bytes 3145732
  220.6 182.4 %copy-start.2 = (bf16[8,128,128]{2,1,0:T(8,128)(2,1)S(1)}, bf16[8,128,128]{2,1,0:T(8,128)(2,1)}, u32[]{:S(2)}) copy-start(bf16[8,128,128]{2,1,0:T(8,128)(2,1)} %param.19) | copy-start | bytes 786436
  222.7 1.7 copy-start.8
  222.7 1.7 copy-start.6
  233.9 1.7 copy-start.8
  233.9 1.7 copy-start.6
  245.3 1.7 copy-start.8
  256.7 1.7 copy-start.8
  268.1 1.7 copy-start.8
  268.1 1.7 copy-start.6
  279.5 1.7 copy-start.8
  279.5 1.7 copy-start.6
  290.9 1.7 copy-start.8
  302.3 1.7 copy-start.8
  313.7 1.7 copy-start.8
  325.1 1.7 copy-start.8
  336.6 1.7 copy-start.8
  336.6 1.7 copy-start.6
  348.0 1.7 copy-start.8
  348.0 1.7 copy-start.6
  359.4 1.7 copy-start.8
  370.8 1.7 copy-start.8
  382.2 1.7 copy-start.8
  393.6 1.7 copy-start.8
  (10 other events, 17.0 us)
where the time goes:
time: 410 us; the launch traced here: 405 us
  blocking collectives  193 us (47%)
  matrix products  119 us (29%)
  other arithmetic  39.3 us (10%)
  local copies, waits for them, and re-layouts  39.2 us (10%)
  starting transfers between devices  13.6 us (3%)
    dot_general x16, matrix products, slot(): jnp.einsum('bts,qbs->qbt', tile, values, preferred_element_type=jnp.float32)  113 us
    all_gather x1, blocking collectives, local(): row_two = lax.all_gather(toward_two[None], 'gy', axis=0, tiled=True)  98.3 us
    all_gather x1, blocking collectives, local(): row_one = lax.all_gather(one_round[None], 'gy', axis=0, tiled=True)  81.5 us
    gather x16, local copies, waits for them, and re-layouts, slot(): sources = jnp.take(places, index, axis=1)  24.2 us
    lt x16, other arithmetic, slot(): live = step < near_count  20.1 us
    all_gather x1, blocking collectives, local(): lax.all_gather(level_three.astype(bf)[None], 'gx', axis=0, tiled=True)  13.3 us
    ppermute x1, starting transfers between devices, extended(): lax.ppermute(head, axis, [((i + 1) % count, i) for i in range(ends)])  11.7 us
    reduce_and x16, other arithmetic, slot(): picked = jnp.take(probe_bf, index, axis=1)  10.9 us
  transfers between devices with their start and end apart: 2, of which 0 were waited for; matrix products, arithmetic and copies ran while one was open for 3% of the time, Pallas kernels for 0%

commit v1 on v0

v1 whole, which is shorter than its diff:
```python
import functools
import math

import jax
import jax.numpy as jnp
from jax import lax
from jax.experimental import pallas as pl
from jax.experimental.pallas import tpu as pltpu
from jax.sharding import PartitionSpec as P

MESH = pl.DeviceIdType.MESH
F32 = jnp.float32
BF = jnp.bfloat16
BOXES = 8
POINTS = 512
PROBES = 16
RANK = 128
NEAR = 16
FAR = 6
WIDTH = BOXES * POINTS
GROUP = 8
ANY = pl.BlockSpec(memory_space=pl.ANY)
VMEM = pl.BlockSpec(memory_space=pltpu.VMEM)
SMEM = pl.BlockSpec(memory_space=pltpu.SMEM)


def dot(a, b):
    return jnp.dot(a, b, preferred_element_type=F32)


def dot_t(a, b):
    return lax.dot_general(a, b, (((1,), (1,)), ((), ())), preferred_element_type=F32)


def gather(ref, index_of):
    return jnp.concatenate([ref[index_of(f)] for f in range(FAR)], axis=1)


def far_kernel(
    gy_count,
    coords,
    vectors,
    basis_hbm,
    leaf_hbm,
    mid_hbm,
    top_hbm,
    one_hbm,
    two_hbm,
    three_hbm,
    far_one,
    far_two,
    far_three,
    side_vec,
    side_pos,
    far_out,
    basis,
    leaf_up,
    mid_up,
    top_up,
    couple_one,
    couple_two,
    couple_three,
    vec,
    pos_f32,
    pos,
    family,
    level_two,
    level_three,
    row_one,
    load_sem,
    side_send,
    side_recv,
    family_send,
    family_recv,
    two_send,
    two_recv,
    row_send,
    row_recv,
    three_send,
    three_recv,
):
    gx = lax.axis_index("gx")
    gy = lax.axis_index("gy")
    group = gy // GROUP
    member = gy % GROUP
    loads = [
        pltpu.make_async_copy(source, target, load_sem.at[n])
        for n, (source, target) in enumerate(
            (
                (basis_hbm, basis),
                (leaf_hbm, leaf_up),
                (mid_hbm, mid_up),
                (top_hbm, top_up),
                (two_hbm.at[group], couple_two),
                (three_hbm, couple_three),
                (one_hbm, couple_one),
            )
        )
    ]
    for load in loads:
        load.start()

    right = (gy + 1) % gy_count
    left = (gy + gy_count - 1) % gy_count

    def in_family(step):
        return group * GROUP + (member + step) % GROUP

    def in_groups(step):
        return ((group + step) % GROUP) * GROUP + member

    barrier = pltpu.get_barrier_semaphore()
    for peer in (left, right):
        pl.semaphore_signal(barrier, inc=1, device_id=(gx, peer), device_id_type=MESH)

    def greet(step, carry):
        for peer in ((gx, in_family(step)), (gx, in_groups(step)), ((gx + step) % 8, gy)):
            pl.semaphore_signal(barrier, inc=1, device_id=peer, device_id_type=MESH)
        return carry

    lax.fori_loop(1, 8, greet, 0)

    vec[...] = vectors[...].astype(BF)
    for comp in range(3):
        for box in range(BOXES):
            row = comp * BOXES + box
            pos_f32[row : row + 1, :] = coords[comp : comp + 1, box * POINTS : (box + 1) * POINTS].astype(F32)
    pos_f32[24:32, :] = jnp.zeros((8, POINTS), F32)
    pos[...] = pos_f32[...].astype(BF)

    loads[0].wait()
    loads[1].wait()
    leaf = jnp.concatenate(
        [dot(vec[:, b * POINTS : (b + 1) * POINTS], basis[b]).astype(BF) for b in range(BOXES)], axis=1
    )
    ups = leaf_up[...].reshape(BOXES * RANK, RANK)
    one = dot(leaf, ups).astype(BF)
    loads[2].wait()
    toward = dot(one, mid_up[0])
    family[member] = jnp.concatenate([one, toward.astype(BF)], axis=0)

    pl.semaphore_wait(barrier, 23)

    def family_copy(step, slot):
        return pltpu.make_async_remote_copy(
            src_ref=family.at[member],
            dst_ref=family.at[member],
            send_sem=family_send.at[step],
            recv_sem=family_recv.at[slot],
            device_id=(gx, in_family(step)),
            device_id_type=MESH,
        )

    def two_copy(step, slot):
        return pltpu.make_async_remote_copy(
            src_ref=level_two.at[group],
            dst_ref=level_two.at[group],
            send_sem=two_send.at[step],
            recv_sem=two_recv.at[slot],
            device_id=(gx, in_groups(step)),
            device_id_type=MESH,
        )

    def row_copy(step, slot):
        part = row_one.at[pl.ds(group * GROUP, GROUP)]
        return pltpu.make_async_remote_copy(
            src_ref=part,
            dst_ref=part,
            send_sem=row_send.at[step],
            recv_sem=row_recv.at[slot],
            device_id=(gx, in_groups(step)),
            device_id_type=MESH,
        )

    def three_copy(step, slot):
        return pltpu.make_async_remote_copy(
            src_ref=level_three.at[gx],
            dst_ref=level_three.at[gx],
            send_sem=three_send.at[step],
            recv_sem=three_recv.at[slot],
            device_id=((gx + step) % 8, gy),
            device_id_type=MESH,
        )

    def start_all(copy, mine):
        def start(step, carry):
            copy(step, mine).start()
            return carry

        lax.fori_loop(1, 8, start, 0)

    def arrive_all(copy, mine):
        def arrive(step, carry):
            copy(step, (mine + step) % 8).wait_recv()
            return carry

        lax.fori_loop(1, 8, arrive, 0)

    def sent_all(copy, mine):
        def sent(step, carry):
            copy(step, mine).wait_send()
            return carry

        lax.fori_loop(1, 8, sent, 0)

    start_all(family_copy, member)

    sides = []
    for n, (source, target) in enumerate(((vec, side_vec), (pos, side_pos))):
        for side, peer in ((0, right), (1, left)):
            sides.append(
                pltpu.make_async_remote_copy(
                    src_ref=source,
                    dst_ref=target.at[side],
                    send_sem=side_send.at[2 * n + side],
                    recv_sem=side_recv.at[2 * n + side],
                    device_id=(gx, peer),
                    device_id_type=MESH,
                )
            )
    for copy in sides:
        copy.start()

    arrive_all(family_copy, member)
    two = jnp.zeros((PROBES, RANK), F32)
    for n in range(GROUP):
        two = two + family[n, PROBES:, :].astype(F32)
        row_one[group * GROUP + n] = family[n, :PROBES, :]
    level_two[group] = two.astype(BF)
    start_all(two_copy, group)
    start_all(row_copy, group)

    loads[3].wait()
    arrive_all(two_copy, group)
    twos = jnp.concatenate([level_two[n] for n in range(8)], axis=1)
    level_three[gx] = dot(twos, top_up[...].reshape(8 * RANK, RANK)).astype(BF)
    start_all(three_copy, gx)

    loads[4].wait()
    local_two = dot(gather(level_two, lambda f: far_two[group, f]), couple_two[...].reshape(FAR * RANK, RANK))
    loads[5].wait()
    loads[6].wait()
    arrive_all(row_copy, group)
    local_one = dot(gather(row_one, lambda f: far_one[0, f]), couple_one[0].reshape(FAR * RANK, RANK))

    arrive_all(three_copy, gx)
    local_three = dot(gather(level_three, lambda f: far_three[0, f]), couple_three[0].reshape(FAR * RANK, RANK))
    local_two = local_two + dot_t(local_three.astype(BF), top_up[group])
    local_one = local_one + dot_t(local_two.astype(BF), mid_up[0])
    local_leaf = dot_t(local_one.astype(BF), ups).astype(BF)
    for b in range(BOXES):
        far_out[:, b * POINTS : (b + 1) * POINTS] = dot_t(local_leaf[:, b * RANK : (b + 1) * RANK], basis[b])

    for copy in sides:
        copy.wait()
    sent_all(family_copy, member)
    sent_all(two_copy, group)
    sent_all(row_copy, group)
    sent_all(three_copy, gx)


def far_field(gy_count, coords, vectors, basis, leaf_up, mid_up, top_up, one, two, three, far_one, far_two, far_three):
    dma = pltpu.SemaphoreType.DMA
    return pl.pallas_call(
        functools.partial(far_kernel, gy_count),
        out_shape=(
            jax.ShapeDtypeStruct((2, PROBES, WIDTH), BF),
            jax.ShapeDtypeStruct((2, 32, POINTS), BF),
            jax.ShapeDtypeStruct((PROBES, WIDTH), F32),
        ),
        in_specs=[VMEM, VMEM] + [ANY] * 7 + [SMEM] * 3,
        out_specs=(ANY, ANY, VMEM),
        scratch_shapes=[
            pltpu.VMEM((BOXES, POINTS, RANK), BF),
            pltpu.VMEM((BOXES, RANK, RANK), BF),
            pltpu.VMEM((1, RANK, RANK), BF),
            pltpu.VMEM((8, RANK, RANK), BF),
            pltpu.VMEM((1, FAR, RANK, RANK), BF),
            pltpu.VMEM((FAR, RANK, RANK), BF),
            pltpu.VMEM((1, FAR, RANK, RANK), BF),
            pltpu.VMEM((PROBES, WIDTH), BF),
            pltpu.VMEM((32, POINTS), F32),
            pltpu.VMEM((32, POINTS), BF),
            pltpu.VMEM((8, 2 * PROBES, RANK), BF),
            pltpu.VMEM((8, PROBES, RANK), BF),
            pltpu.VMEM((8, PROBES, RANK), BF),
            pltpu.VMEM((64, PROBES, RANK), BF),
            dma((7,)),
            dma((4,)),
            dma((4,)),
            dma((8,)),
            dma((8,)),
            dma((8,)),
            dma((8,)),
            dma((8,)),
            dma((8,)),
            dma((8,)),
            dma((8,)),
        ],
        compiler_params=pltpu.CompilerParams(
            collective_id=0, has_side_effects=True, vmem_limit_bytes=40 << 20
        ),
    )(coords, vectors, basis, leaf_up, mid_up, top_up, one, two, three, far_one, far_two, far_three)


def lanes(box):
    return pl.ds(pl.multiple_of(box * POINTS, POINTS), POINTS)


def near_kernel(
    gy_count,
    near_list,
    near_count,
    coords,
    vectors,
    side_vec,
    side_pos,
    far_part,
    out,
    pos,
    raw,
    source,
    target,
    vec,
    dist,
    times,
    task_box,
    task_from,
):
    gy = lax.axis_index("gy")

    def clear(n, carry):
        for k in range(8):
            times[n * 8 + k] = 0
        return carry

    lax.fori_loop(0, 24, clear, 0)
    tasks = jnp.int32(0)
    for box in range(BOXES):

        def add(slot, tasks, box=box):
            place = near_list[box, slot]
            column = gy + place // BOXES - 1
            known = times[box * 24 + place]
            times[box * 24 + place] = known + 1
            task_box[tasks] = box
            task_from[tasks] = place
            fresh = (known == 0) & (column >= 0) & (column < gy_count)
            return tasks + jnp.where(fresh, 1, 0)

        tasks = lax.fori_loop(0, near_count[box], add, tasks)
    for k in range(4):
        task_box[tasks + k] = 0
        task_from[tasks + k] = BOXES

    for comp in range(3):
        for box in range(BOXES):
            row = comp * BOXES + box
            pos[1, row : row + 1, :] = coords[comp : comp + 1, box * POINTS : (box + 1) * POINTS].astype(F32)
    pos[0] = side_pos[0].astype(F32)
    pos[2] = side_pos[1].astype(F32)
    raw[...] = jnp.zeros_like(raw)
    ones = jnp.ones((3, WIDTH), F32)
    for third in range(3):
        parts = [pos[third, comp * BOXES : (comp + 1) * BOXES, :] for comp in range(3)]
        norm = parts[0] * parts[0] + parts[1] * parts[1] + parts[2] * parts[2]
        high = norm.astype(BF).astype(F32)
        rest = norm - high
        middle = rest.astype(BF).astype(F32)
        low = rest - middle
        rows = [-2.0 * part for part in parts] + [high, middle, low]
        for box in range(BOXES):
            for n, value in enumerate(rows):
                raw[n : n + 1, box * POINTS : (box + 1) * POINTS] = value[box : box + 1, :]
        raw[6:9, :] = ones
        source[:, third * WIDTH : (third + 1) * WIDTH] = raw[...].astype(BF)
        if third == 1:
            for box in range(BOXES):
                for n, value in enumerate(parts):
                    raw[n : n + 1, box * POINTS : (box + 1) * POINTS] = value[box : box + 1, :]
                for n, value in enumerate((high, middle, low)):
                    raw[n + 6 : n + 7, box * POINTS : (box + 1) * POINTS] = value[box : box + 1, :]
            raw[3:6, :] = ones
            target[...] = raw[...].astype(BF)
    vec[:, :WIDTH] = side_vec[0]
    vec[:, WIDTH : 2 * WIDTH] = vectors[...].astype(BF)
    vec[:, 2 * WIDTH :] = side_vec[1]

    out[...] = far_part[...]

    def squares(task):
        return lax.dot_general(
            source[:, lanes(task_from[task])],
            target[:, lanes(task_box[task])],
            (((0,), (0,)), ((), ())),
            preferred_element_type=F32,
        )

    dist[0] = squares(0)

    def step(turn, carry):
        for k in range(4):
            task = turn * 4 + k
            square = jnp.maximum(dist[k % 2], 1e-30)
            dist[1 - k % 2] = squares(task + 1)
            tile = jnp.exp2((square * -math.log2(math.e)) * lax.rsqrt(square)).astype(BF)
            box = task_box[task]
            place = task_from[task]
            count = jnp.where(task < tasks, times[box * 24 + place], 0)
            weight = count.astype(F32) * POINTS**-0.5
            out[:, lanes(box)] += weight * dot(vec[:, lanes(place)], tile)
        return carry

    lax.fori_loop(0, (tasks + 3) // 4, step, 0)


def near_field(gy_count, near_list, near_count, coords, vectors, side_vec, side_pos, far_part):
    return pl.pallas_call(
        functools.partial(near_kernel, gy_count),
        out_shape=jax.ShapeDtypeStruct((PROBES, WIDTH), F32),
        in_specs=[SMEM, SMEM] + [VMEM] * 5,
        out_specs=VMEM,
        scratch_shapes=[
            pltpu.VMEM((3, 32, POINTS), F32),
            pltpu.VMEM((16, WIDTH), F32),
            pltpu.VMEM((16, 3 * WIDTH), BF),
            pltpu.VMEM((16, WIDTH), BF),
            pltpu.VMEM((PROBES, 3 * WIDTH), BF),
            pltpu.VMEM((2, POINTS, POINTS), F32),
            pltpu.SMEM((192,), jnp.int32),
            pltpu.SMEM((136,), jnp.int32),
            pltpu.SMEM((136,), jnp.int32),
        ],
        compiler_params=pltpu.CompilerParams(vmem_limit_bytes=40 << 20),
    )(near_list, near_count, coords, vectors, side_vec, side_pos, far_part)


def local(gy_count, *args):
    coords, vectors, basis, leaf_up, mid_up, top_up = args[:6]
    couple_one, couple_two, couple_three, far_one, far_two, far_three, near_list, near_count = args[6:]
    side_vec, side_pos, far_part = far_field(
        gy_count,
        coords,
        vectors,
        basis,
        leaf_up,
        mid_up,
        top_up,
        couple_one,
        couple_two,
        couple_three,
        far_one,
        far_two,
        far_three,
    )
    return near_field(gy_count, near_list, near_count, coords, vectors, side_vec, side_pos, far_part)


def solution(mesh):
    both = ("gx", "gy")
    return jax.shard_map(
        functools.partial(local, mesh.shape["gy"]),
        mesh=mesh,
        in_specs=(
            P(None, both),
            P(None, both),
            P(both, None, None),
            P(both, None, None),
            P(both, None, None),
            P("gx", None, None),
            P(both, None, None, None),
            P("gx", None, None, None),
            P("gx", None, None, None),
            P(both, None),
            P("gx", None),
            P("gx", None),
            P(both, None),
            P(both),
        ),
        out_specs=P(None, both),
        check_vma=False,
    )
```

time: 410 us -> 76.8 us (0.19)
  the two profiles are of different devices: /device:TPU:6 before, /device:TPU:68 now
where the time goes in v1:
time: 76.8 us; the launch traced here: 76.2 us
  Pallas kernels  65.4 us (85%)
  local copies, waits for them, and re-layouts  10.9 us (14%)
    pallas_call x1, Pallas kernels, far_field(): pl.pallas_call(functools.partial(far_kernel, gy_count), out_shape=(jax.Sh...  39.7 us
    pallas_call x1, Pallas kernels, near_field(): pl.pallas_call(functools.partial(near_kernel, gy_count), out_shape=jax.Sh...  25.7 us
    unnamed x28, local copies, waits for them, and re-layouts  10.9 us

profile of v1, /device:TPU:68, one launch (start us, length us, event | category | flops | bytes accessed | tf_op | source)
XLA Modules:
  0.0 76.2 jit_solution(432639243155296549)
XLA Ops:
  0.0 0.0 copy-start
  0.0 1.4 %copy-done = bf16[8,6,128,128]{3,2,1,0:T(8,128)(2,1)S(1)} copy-done((bf16[8,6,128,128]{3,2,1,0:T(8,128)(2,1)S(1)}, bf16[8,6,128,128]{3,2,1,0:T(8,128)(2,1)}, u32[]{:S(2)}) %copy-start) | copy-done | bytes 1572888
  1.4 0.0 copy-start.1
  1.4 1.2 %copy-done.1 = bf16[8,512,128]{2,1,0:T(8,128)(2,1)S(1)} copy-done((bf16[8,512,128]{2,1,0:T(8,128)(2,1)S(1)}, bf16[8,512,128]{2,1,0:T(8,128)(2,1)}, u32[]{:S(2)}) %copy-start.1) | copy-done | bytes 1048600
  2.6 0.0 copy-start.2
  2.6 0.9 %copy-done.2 = f32[16,4096]{1,0:T(8,128)S(1)} copy-done((f32[16,4096]{1,0:T(8,128)S(1)}, f32[16,4096]{1,0:T(8,128)}, u32[]{:S(2)}) %copy-start.2) | copy-done | bytes 262168
  3.6 0.0 copy-start.3
  3.6 0.9 %copy-done.3 = bf16[8,128,128]{2,1,0:T(8,128)(2,1)S(1)} copy-done((bf16[8,128,128]{2,1,0:T(8,128)(2,1)S(1)}, bf16[8,128,128]{2,1,0:T(8,128)(2,1)}, u32[]{:S(2)}) %copy-start.3) | copy-done | bytes 262168
  4.5 0.0 copy-start.4
  4.5 0.9 %copy-done.4 = bf16[8,128,128]{2,1,0:T(8,128)(2,1)S(1)} copy-done((bf16[8,128,128]{2,1,0:T(8,128)(2,1)S(1)}, bf16[8,128,128]{2,1,0:T(8,128)(2,1)}, u32[]{:S(2)}) %copy-start.4) | copy-done | bytes 262168
  5.5 0.0 copy-start.5
  5.5 0.9 %copy-done.5 = bf16[1,6,128,128]{3,2,1,0:T(8,128)(2,1)S(1)} copy-done((bf16[1,6,128,128]{3,2,1,0:T(8,128)(2,1)S(1)}, bf16[1,6,128,128]{3,2,1,0:T(8,128)(2,1)}, u32[]{:S(2)}) %copy-start.5) | copy-done | bytes 196632
  6.4 0.0 copy-start.6
  6.4 0.9 %copy-done.6 = bf16[1,6,128,128]{3,2,1,0:T(8,128)(2,1)S(1)} copy-done((bf16[1,6,128,128]{3,2,1,0:T(8,128)(2,1)S(1)}, bf16[1,6,128,128]{3,2,1,0:T(8,128)(2,1)}, u32[]{:S(2)}) %copy-start.6) | copy-done | bytes 196632
  7.3 0.0 copy-start.7
  7.3 0.8 copy-done.7
  8.1 0.0 copy-start.8
  8.1 0.8 copy-done.8
  8.9 0.0 copy-start.9
  8.9 0.7 copy-done.9
  9.5 0.0 copy-start.11
  9.5 0.7 copy-done.11
  10.2 0.0 copy-start.12
  10.2 0.7 copy-done.12
  10.9 0.0 copy-start.10
  10.9 0.0 copy-start.13
  10.9 39.7 %shard_map.136 = (bf16[2,16,4096]{2,1,0:T(8,128)(2,1)S(1)}, bf16[2,32,512]{2,1,0:T(8,128)(2,1)S(1)}, f32[16,4096]{1,0:T(8,128)S(1)}) custom-call(bf16[3,4096]{1,0:T(4,128)(2,1)S(1)} %copy-done.7, f32[16,4096]{1,0:T(8,128)S(1)} %copy-done.2, bf16[8,512,128]{2,1,0:T(8,128)(2,1)S(1)} %copy-done.1, bf16[8,128,128]{2,1,0:T(8,128)(2,1)S(1)} %copy-done.3, ...), custom_call_target="tpu_custom_call" | custom-call | tf_op jit(solution)/shard_map/pallas_call | solution.py:264
  50.6 0.0 copy-done.10
  50.6 0.0 copy-done.13
  50.6 25.7 %shard_map.137 = f32[16,4096]{1,0:T(8,128)} custom-call(s32[8,16]{1,0:T(8,128)S(1)} %copy-done.10, s32[8]{0:T(128)S(1)} %copy-done.13, bf16[3,4096]{1,0:T(4,128)(2,1)S(1)} %copy-done.7, f32[16,4096]{1,0:T(8,128)S(1)} %copy-done.2, bf16[2,16,4096]{2,1,0:T(8,128)(2,1)S(1)} %get-tuple-element.8.side_vec, bf16[2,32,512]{2,1,0:T(8,128)(2,1)S(1)} %get-tuple-element.9.side_pos, ...), custom_call_target="tpu_custom_call" | custom-call | tf_op jit(solution)/shard_map/pallas_call | solution.py:418
Async XLA Ops:
  0.0 1.4 %copy-start = (bf16[8,6,128,128]{3,2,1,0:T(8,128)(2,1)S(1)}, bf16[8,6,128,128]{3,2,1,0:T(8,128)(2,1)}, u32[]{:S(2)}) copy-start(bf16[8,6,128,128]{3,2,1,0:T(8,128)(2,1)} %two_hbm.1) | copy-start | bytes 4718596
  1.4 1.2 %copy-start.1 = (bf16[8,512,128]{2,1,0:T(8,128)(2,1)S(1)}, bf16[8,512,128]{2,1,0:T(8,128)(2,1)}, u32[]{:S(2)}) copy-start(bf16[8,512,128]{2,1,0:T(8,128)(2,1)} %basis_hbm.1) | copy-start | bytes 3145732
  2.6 0.9 %copy-start.2 = (f32[16,4096]{1,0:T(8,128)S(1)}, f32[16,4096]{1,0:T(8,128)}, u32[]{:S(2)}) copy-start(f32[16,4096]{1,0:T(8,128)} %vectors.3) | copy-start | bytes 786436
  3.6 0.9 %copy-start.3 = (bf16[8,128,128]{2,1,0:T(8,128)(2,1)S(1)}, bf16[8,128,128]{2,1,0:T(8,128)(2,1)}, u32[]{:S(2)}) copy-start(bf16[8,128,128]{2,1,0:T(8,128)(2,1)} %leaf_hbm.1) | copy-start | bytes 786436
  4.5 0.9 %copy-start.4 = (bf16[8,128,128]{2,1,0:T(8,128)(2,1)S(1)}, bf16[8,128,128]{2,1,0:T(8,128)(2,1)}, u32[]{:S(2)}) copy-start(bf16[8,128,128]{2,1,0:T(8,128)(2,1)} %top_hbm.1) | copy-start | bytes 786436
  5.5 0.9 %copy-start.5 = (bf16[1,6,128,128]{3,2,1,0:T(8,128)(2,1)S(1)}, bf16[1,6,128,128]{3,2,1,0:T(8,128)(2,1)}, u32[]{:S(2)}) copy-start(bf16[1,6,128,128]{3,2,1,0:T(8,128)(2,1)} %one_hbm.1) | copy-start | bytes 589828
  6.4 0.9 %copy-start.6 = (bf16[1,6,128,128]{3,2,1,0:T(8,128)(2,1)S(1)}, bf16[1,6,128,128]{3,2,1,0:T(8,128)(2,1)}, u32[]{:S(2)}) copy-start(bf16[1,6,128,128]{3,2,1,0:T(8,128)(2,1)} %three_hbm.1) | copy-start | bytes 589828
  7.3 0.8 copy-start.7
  8.1 0.8 copy-start.8
  8.9 0.7 copy-start.9
  9.5 0.7 copy-start.11
  10.2 0.7 copy-start.12
  10.9 39.7 %copy-start.10 = (s32[8,16]{1,0:T(8,128)S(1)}, s32[8,16]{1,0:T(8,128)}, u32[]{:S(2)}) copy-start(s32[8,16]{1,0:T(8,128)} %near_list.1) | copy-start | bytes 1540
  10.9 39.7 %copy-start.13 = (s32[8]{0:T(128)S(1)}, s32[8]{0:T(128)}, u32[]{:S(2)}) copy-start(s32[8]{0:T(128)} %near_count.1) | copy-start | bytes 100

commit v2 on v0

v2 whole, which is shorter than its diff:
```python
import functools
import math

import jax
import jax.numpy as jnp
from jax import lax
from jax.experimental import pallas as pl
from jax.experimental.pallas import tpu as pltpu
from jax.sharding import PartitionSpec as P

MESH = pl.DeviceIdType.MESH
F32 = jnp.float32
BF = jnp.bfloat16
I32 = jnp.int32
BOXES = 8
POINTS = 512
PROBES = 16
RANK = 128
NEAR = 16
FAR = 6
WIDTH = BOXES * POINTS
GX = 8
LINE = 16
LINES = 4
GROUP = 8
TURN = 4
OWN_TURNS = 7
MID_TURNS = 2
LAST_TURNS = 2
OWN_DONE = OWN_TURNS * TURN
SIDE_DONE = (MID_TURNS + LAST_TURNS) * TURN
SCALE = POINTS**-0.5
VMEM_LIMIT = 63 << 20
HBM = pl.BlockSpec(memory_space=pltpu.HBM)
VMEM = pl.BlockSpec(memory_space=pltpu.VMEM)
SMEM = pl.BlockSpec(memory_space=pltpu.SMEM)


def dot(a, b):
    return jnp.dot(a, b, preferred_element_type=F32)


def dot_t(a, b):
    return lax.dot_general(a, b, (((1,), (1,)), ((), ())), preferred_element_type=F32)


def span(box):
    return slice(box * POINTS, (box + 1) * POINTS)


def gather(ref, index_of):
    return jnp.concatenate([ref[index_of(f)] for f in range(FAR)], axis=1)


def squares(source, target):
    return lax.dot_general(source, target, (((0,), (0,)), ((), ())), preferred_element_type=F32)


def tile_of(square):
    square = jnp.maximum(square, 1e-30)
    return jnp.exp2((square * -math.log2(math.e)) * lax.rsqrt(square)).astype(BF)


def norm_parts(parts):
    norm = parts[0] * parts[0] + parts[1] * parts[1] + parts[2] * parts[2]
    high = norm.astype(BF).astype(F32)
    rest = norm - high
    middle = rest.astype(BF).astype(F32)
    return [high, middle, rest - middle]


def set_rows(raw, first, values):
    for n, value in enumerate(values):
        for box in range(BOXES):
            raw[box, first + n : first + n + 1, :] = value[box : box + 1, :]


def compact(times, box, place):
    count = times.shape[0]
    across = lax.broadcasted_iota(I32, (count, 128), 1)
    down = lax.broadcasted_iota(I32, (count, 128), 0)
    live = jnp.broadcast_to(jnp.where(times > 0, 1, 0), (count, 128))
    along = jnp.sum(jnp.where(across == down, live, 0), axis=0, keepdims=True)
    rank = jnp.sum(jnp.where(across < down, along, 0), axis=1, keepdims=True)
    hit = (rank == across) & (live > 0)
    rows = [jnp.sum(jnp.where(hit, value, 0), axis=0, keepdims=True) for value in (box, place, times)]
    return rows, jnp.sum(live, axis=0, keepdims=True)


def pair_lists(near_list, near_count, gy, gy_count, out):
    place = lax.broadcasted_iota(I32, (3 * BOXES, NEAR), 0)
    slot = lax.broadcasted_iota(I32, (3 * BOXES, NEAR), 1)
    column = gy + place // BOXES - 1
    inside = (column >= 0) & (column < gy_count)
    own, side = [], []
    for box in range(BOXES):
        named = (near_list[box : box + 1, :] == place) & (slot < near_count[box]) & inside
        times = jnp.sum(jnp.where(named, 1, 0), axis=1, keepdims=True)
        own.append(times[BOXES : 2 * BOXES])
        side += [times[:BOXES], times[2 * BOXES :]]
    own, side = jnp.concatenate(own, axis=0), jnp.concatenate(side, axis=0)
    n = lax.broadcasted_iota(I32, own.shape, 0)
    own_rows, own_count = compact(own, n // BOXES, n % BOXES)
    n = lax.broadcasted_iota(I32, side.shape, 0)
    side_rows, side_count = compact(side, n // (2 * BOXES), n % (2 * BOXES))
    for n, row in enumerate(own_rows + side_rows + [own_count, side_count]):
        out[n : n + 1, :] = row


def far_kernel(
    gy_count,
    coords_hbm,
    vectors_hbm,
    list_hbm,
    count_hbm,
    basis_hbm,
    leaf_hbm,
    mid_hbm,
    top_hbm,
    one_hbm,
    two_hbm,
    three_hbm,
    far_one_hbm,
    far_two_hbm,
    far_three_hbm,
    total,
    pairs,
    own_vec,
    side_vec,
    own_source,
    side_source,
    target,
    coords,
    vectors,
    near_list,
    near_count,
    basis,
    leaf_up,
    mid_up,
    top_up,
    couple_one,
    couple_two,
    couple_three,
    far_one,
    far_two,
    far_three,
    pos_f32,
    pos,
    side_pos,
    raw,
    dist,
    tasks,
    toward,
    level_two,
    level_three,
    row_one,
    load_sem,
    task_sem,
    side_send,
    side_recv,
    toward_send,
    toward_recv,
    line_send,
    line_recv,
    two_send,
    two_recv,
    row_send,
    row_recv,
    three_send,
    three_recv,
):
    gx = lax.axis_index("gx")
    gy = lax.axis_index("gy")
    x = gy // LINE
    z = gy % LINE
    group = gy // GROUP
    loads = [
        pltpu.make_async_copy(source, goal, load_sem.at[n])
        for n, (source, goal) in enumerate(
            (
                (vectors_hbm, vectors),
                (coords_hbm, coords),
                (list_hbm, near_list),
                (count_hbm, near_count),
                (basis_hbm, basis),
                (leaf_hbm, leaf_up),
                (mid_hbm, mid_up),
                (top_hbm, top_up),
                (two_hbm.at[group], couple_two),
                (three_hbm, couple_three),
                (one_hbm, couple_one),
                (far_one_hbm, far_one),
                (far_two_hbm, far_two),
                (far_three_hbm, far_three),
            )
        )
    ]
    for load in loads:
        load.start()

    right = (gy + 1) % gy_count
    left = (gy + gy_count - 1) % gy_count

    def in_line(step):
        return x * LINE + (z + step) % LINE

    def in_plane(step):
        return ((x + step) % LINES) * LINE + z

    barrier = pltpu.get_barrier_semaphore()

    def greet(peer):
        pl.semaphore_signal(barrier, inc=1, device_id=peer, device_id_type=MESH)

    def greet_line(n, carry):
        greet((gx, in_line(n)))
        return carry

    def greet_three(n, carry):
        greet(((gx + n) % GX, gy))
        return carry

    lax.fori_loop(1, LINE, greet_line, 0)
    for n in range(1, LINES):
        greet((gx, in_plane(n)))
    lax.fori_loop(1, GX, greet_three, 0)
    greet((gx, left))
    greet((gx, right))

    loads[0].wait()
    for box in range(BOXES):
        own_vec[box] = vectors[:, span(box)].astype(BF)
    loads[4].wait()
    loads[5].wait()
    leaf = jnp.concatenate([dot(own_vec[b], basis[b]).astype(BF) for b in range(BOXES)], axis=1)
    ups = leaf_up[...].reshape(BOXES * RANK, RANK)
    one = dot(leaf, ups).astype(BF)
    row_one[gy] = one
    loads[6].wait()
    toward[z] = dot(one, mid_up[0]).astype(BF)

    loads[1].wait()
    for comp in range(3):
        for box in range(BOXES):
            row = comp * BOXES + box
            pos_f32[row : row + 1, :] = coords[comp : comp + 1, span(box)].astype(F32)
    pos_f32[24:32, :] = jnp.zeros((8, POINTS), F32)
    pos[...] = pos_f32[...].astype(BF)
    loads[2].wait()
    loads[3].wait()
    pair_lists(near_list, near_count, gy, gy_count, pairs)
    task_copy = pltpu.make_async_copy(pairs, tasks, task_sem.at[0])
    task_copy.start()

    raw[...] = jnp.zeros_like(raw)
    ones = [jnp.ones((BOXES, POINTS), F32)] * 3
    parts = [pos_f32[n * BOXES : (n + 1) * BOXES, :] for n in range(3)]
    norms = norm_parts(parts)
    set_rows(raw, 0, parts + ones + norms)
    target[...] = raw[...].astype(BF)
    set_rows(raw, 0, [-2.0 * part for part in parts] + norms + ones)
    own_source[...] = raw[...].astype(BF)
    total[...] = jnp.zeros_like(total)
    task_copy.wait()

    def begin(first_row, source_ref, task):
        dist[0] = squares(source_ref[tasks[first_row + 1, task]], target[tasks[first_row, task]])

    def fill(first_row, source_ref, vec_ref, first, last):
        def turn(n, carry):
            for k in range(TURN):
                task = n * TURN + k
                square = dist[k % 2]
                dist[1 - k % 2] = squares(
                    source_ref[tasks[first_row + 1, task + 1]], target[tasks[first_row, task + 1]]
                )
                part = dot(vec_ref[tasks[first_row + 1, task]], tile_of(square))
                box = tasks[first_row, task]
                weight = tasks[first_row + 2, task].astype(F32) * SCALE
                for b in range(BOXES):
                    total[:, span(b)] += jnp.where(box == b, weight, 0.0) * part
            return carry

        lax.fori_loop(first, last, turn, 0)

    ahead = (1 - z // 8) * (OWN_TURNS - z // 2) + z // 14
    begin(0, own_source, 0)
    fill(0, own_source, own_vec, 0, ahead)

    pl.semaphore_wait(barrier, LINE - 1 + LINES - 1 + GX - 1 + 2)

    def send(ref, sends, recvs, step, slot, peer):
        return pltpu.make_async_remote_copy(
            src_ref=ref,
            dst_ref=ref,
            send_sem=sends.at[step],
            recv_sem=recvs.at[slot],
            device_id=peer,
            device_id_type=MESH,
        )

    def toward_copy(step, slot):
        return send(toward.at[z], toward_send, toward_recv, step, slot, (gx, in_line(step)))

    def line_copy(step, slot):
        return send(row_one.at[gy], line_send, line_recv, step, slot, (gx, in_line(step)))

    def two_copy(step, slot):
        return send(level_two.at[x], two_send, two_recv, step, slot, (gx, in_plane(step)))

    def row_copy(step, slot):
        part = row_one.at[pl.ds(x * LINE, LINE)]
        return send(part, row_send, row_recv, step, slot, (gx, in_plane(step)))

    def three_copy(step, slot):
        return send(level_three.at[gx], three_send, three_recv, step, slot, ((gx + step) % GX, gy))

    def each(count, do):
        def body(n, carry):
            do(n)
            return carry

        lax.fori_loop(1, count, body, 0)

    def start_all(copy, mine, count):
        each(count, lambda n: copy(n, mine).start())

    def start_far_first(copy, mine):
        for n in (8, 7, 9, 6, 10, 5, 11, 4, 12, 3, 13, 2, 14, 1, 15):
            copy(n, mine).start()

    def arrive_all(copy, mine, count):
        each(count, lambda n: copy(n, (mine + n) % count).wait_recv())

    def sent_all(copy, mine, count):
        each(count, lambda n: copy(n, mine).wait_send())

    start_far_first(toward_copy, z)
    sides = []
    for n, (source, goal, rows) in enumerate(((own_vec, side_vec, 8), (pos, side_pos, 32))):
        for side, peer in ((0, right), (1, left)):
            sides.append(
                pltpu.make_async_remote_copy(
                    src_ref=source,
                    dst_ref=goal.at[pl.ds(side * rows, rows)],
                    send_sem=side_send.at[2 * n + side],
                    recv_sem=side_recv.at[2 * n + side],
                    device_id=(gx, peer),
                    device_id_type=MESH,
                )
            )
    for copy in sides:
        copy.start()
    start_far_first(line_copy, z)

    fill(0, own_source, own_vec, ahead, OWN_TURNS)

    arrive_all(toward_copy, z, LINE)
    for half in range(2):
        two = jnp.zeros((PROBES, RANK), F32)
        for n in range(GROUP):
            two = two + toward[half * GROUP + n].astype(F32)
        level_two[x, half] = two.astype(BF)
    start_all(two_copy, x, LINES)
    arrive_all(line_copy, z, LINE)
    start_all(row_copy, x, LINES)

    for copy in sides:
        copy.wait_recv()
    for side in range(2):
        first = side * 32
        near = side_pos[first : first + 24, :].astype(F32)
        parts = [near[n * BOXES : (n + 1) * BOXES, :] for n in range(3)]
        set_rows(raw, 0, [-2.0 * part for part in parts] + norm_parts(parts))
        side_source[side * BOXES : (side + 1) * BOXES] = raw[...].astype(BF)
    begin(3, side_source, 0)
    fill(3, side_source, side_vec, 0, MID_TURNS)

    loads[7].wait()
    arrive_all(two_copy, x, LINES)
    twos = jnp.concatenate([level_two[n // 2, n % 2] for n in range(8)], axis=1)
    level_three[gx] = dot(twos, top_up[...].reshape(8 * RANK, RANK)).astype(BF)
    start_all(three_copy, gx, GX)

    for load in loads[8:]:
        load.wait()
    source_two = gather(level_two, lambda f: (far_two[group, f] // 2, far_two[group, f] % 2))
    local_two = dot(source_two, couple_two[...].reshape(FAR * RANK, RANK))
    arrive_all(row_copy, x, LINES)
    local_one = dot(gather(row_one, lambda f: far_one[0, f]), couple_one[0].reshape(FAR * RANK, RANK))
    fill(3, side_source, side_vec, MID_TURNS, MID_TURNS + LAST_TURNS)

    arrive_all(three_copy, gx, GX)
    local_three = dot(gather(level_three, lambda f: far_three[0, f]), couple_three[0].reshape(FAR * RANK, RANK))
    local_two = local_two + dot_t(local_three.astype(BF), top_up[group])
    local_one = local_one + dot_t(local_two.astype(BF), mid_up[0])
    local_leaf = dot_t(local_one.astype(BF), ups).astype(BF)
    for b in range(BOXES):
        total[:, span(b)] += dot_t(local_leaf[:, b * RANK : (b + 1) * RANK], basis[b])

    for copy in sides:
        copy.wait_send()
    sent_all(toward_copy, z, LINE)
    sent_all(line_copy, z, LINE)
    sent_all(two_copy, x, LINES)
    sent_all(row_copy, x, LINES)
    sent_all(three_copy, gx, GX)


def far_field(gy_count, *arrays):
    dma = pltpu.SemaphoreType.DMA
    boxes = (BOXES, PROBES, POINTS)
    sides = (2 * BOXES, PROBES, POINTS)
    return pl.pallas_call(
        functools.partial(far_kernel, gy_count),
        out_shape=(
            jax.ShapeDtypeStruct((PROBES, WIDTH), F32),
            jax.ShapeDtypeStruct((8, 128), I32),
            jax.ShapeDtypeStruct(boxes, BF),
            jax.ShapeDtypeStruct(sides, BF),
            jax.ShapeDtypeStruct(boxes, BF),
            jax.ShapeDtypeStruct(sides, BF),
            jax.ShapeDtypeStruct(boxes, BF),
        ),
        in_specs=[HBM] * 14,
        out_specs=(VMEM,) * 7,
        scratch_shapes=[
            pltpu.VMEM((3, WIDTH), BF),
            pltpu.VMEM((PROBES, WIDTH), F32),
            pltpu.VMEM((BOXES, NEAR), I32),
            pltpu.SMEM((BOXES,), I32),
            pltpu.VMEM((BOXES, POINTS, RANK), BF),
            pltpu.VMEM((BOXES, RANK, RANK), BF),
            pltpu.VMEM((1, RANK, RANK), BF),
            pltpu.VMEM((8, RANK, RANK), BF),
            pltpu.VMEM((1, FAR, RANK, RANK), BF),
            pltpu.VMEM((FAR, RANK, RANK), BF),
            pltpu.VMEM((1, FAR, RANK, RANK), BF),
            pltpu.SMEM((1, FAR), I32),
            pltpu.SMEM((8, FAR), I32),
            pltpu.SMEM((1, FAR), I32),
            pltpu.VMEM((32, POINTS), F32),
            pltpu.VMEM((32, POINTS), BF),
            pltpu.VMEM((64, POINTS), BF),
            pltpu.VMEM(boxes, F32),
            pltpu.VMEM((2, POINTS, POINTS), F32),
            pltpu.SMEM((8, 128), I32),
            pltpu.VMEM((LINE, PROBES, RANK), BF),
            pltpu.VMEM((LINES, 2, PROBES, RANK), BF),
            pltpu.VMEM((GX, PROBES, RANK), BF),
            pltpu.VMEM((LINE * LINES, PROBES, RANK), BF),
            dma((14,)),
            dma((1,)),
            dma((4,)),
            dma((4,)),
            dma((LINE,)),
            dma((LINE,)),
            dma((LINE,)),
            dma((LINE,)),
            dma((LINES,)),
            dma((LINES,)),
            dma((LINES,)),
            dma((LINES,)),
            dma((GX,)),
            dma((GX,)),
        ],
        compiler_params=pltpu.CompilerParams(
            collective_id=0, has_side_effects=True, vmem_limit_bytes=VMEM_LIMIT
        ),
    )(*arrays)


def near_kernel(pairs, total_hbm, own_vec, side_vec, own_source, side_source, target_hbm, out, vec, source, target, dist, sem):
    loads = [
        pltpu.make_async_copy(a, b, sem.at[n])
        for n, (a, b) in enumerate(
            (
                (own_source, source.at[pl.ds(0, BOXES)]),
                (side_source, source.at[pl.ds(BOXES, 2 * BOXES)]),
                (target_hbm, target),
                (own_vec, vec.at[pl.ds(0, BOXES)]),
                (side_vec, vec.at[pl.ds(BOXES, 2 * BOXES)]),
                (total_hbm, out),
            )
        )
    ]
    for load in loads:
        load.start()
    own = jnp.maximum(pairs[6, 0] - OWN_DONE, 0)
    tasks = own + jnp.maximum(pairs[7, 0] - SIDE_DONE, 0)

    def find(task):
        mine = task < own
        row = jnp.where(mine, 0, 3)
        lane = jnp.minimum(jnp.where(mine, OWN_DONE + task, SIDE_DONE + task - own), 127)
        place = pairs[row + 1, lane] + jnp.where(mine, 0, BOXES)
        return pairs[row, lane], place, jnp.where(task < tasks, pairs[row + 2, lane], 0)

    for load in loads:
        load.wait()

    def measure(task):
        box, place, _ = find(task)
        return squares(source[place], target[box])

    dist[0] = measure(0)

    def turn(n, carry):
        for k in range(TURN):
            task = n * TURN + k
            square = dist[k % 2]
            dist[1 - k % 2] = measure(task + 1)
            box, place, times = find(task)
            lanes = pl.ds(pl.multiple_of(box * POINTS, POINTS), POINTS)
            out[:, lanes] += (times.astype(F32) * SCALE) * dot(vec[place], tile_of(square))
        return carry

    lax.fori_loop(0, (tasks + TURN - 1) // TURN, turn, 0)


def near_field(total, pairs, *arrays):
    return pl.pallas_call(
        near_kernel,
        out_shape=jax.ShapeDtypeStruct((PROBES, WIDTH), F32),
        in_specs=[SMEM] + [HBM] * 6,
        out_specs=VMEM,
        scratch_shapes=[
            pltpu.VMEM((3 * BOXES, PROBES, POINTS), BF),
            pltpu.VMEM((3 * BOXES, PROBES, POINTS), BF),
            pltpu.VMEM((BOXES, PROBES, POINTS), BF),
            pltpu.VMEM((2, POINTS, POINTS), F32),
            pltpu.SemaphoreType.DMA((6,)),
        ],
        compiler_params=pltpu.CompilerParams(vmem_limit_bytes=VMEM_LIMIT),
    )(pairs, total, *arrays)


def local(gy_count, coords, vectors, *rest):
    matrices, near_list, near_count = rest[:-2], rest[-2], rest[-1]
    return near_field(*far_field(gy_count, coords, vectors, near_list, near_count, *matrices))


def solution(mesh):
    both = ("gx", "gy")
    return jax.shard_map(
        functools.partial(local, mesh.shape["gy"]),
        mesh=mesh,
        in_specs=(
            P(None, both),
            P(None, both),
            P(both, None, None),
            P(both, None, None),
            P(both, None, None),
            P("gx", None, None),
            P(both, None, None, None),
            P("gx", None, None, None),
            P("gx", None, None, None),
            P(both, None),
            P("gx", None),
            P("gx", None),
            P(both, None),
            P(both),
        ),
        out_specs=P(None, both),
        check_vma=False,
    )
```

time: 410 us -> 53.9 us (0.13)
  the two profiles are of different devices: /device:TPU:6 before, /device:TPU:64 now
where the time goes in v2:
time: 53.9 us; the launch traced here: 53.7 us
  Pallas kernels  53.7 us (100%)
    pallas_call x1, Pallas kernels, far_field(): pl.pallas_call(functools.partial(far_kernel, gy_count), out_shape=(jax.Sh...  38.4 us
    pallas_call x1, Pallas kernels, near_field(): pl.pallas_call(near_kernel, out_shape=jax.ShapeDtypeStruct((PROBES, WIDTH...  15.4 us

profile of v2, /device:TPU:64, one launch (start us, length us, event | category | flops | bytes accessed | tf_op | source)
XLA Modules:
  0.0 53.7 jit_solution(1088678261249987018)
XLA Ops:
  0.0 38.4 %shard_map.136 = (f32[16,4096]{1,0:T(8,128)}, s32[8,128]{1,0:T(8,128)}, bf16[8,16,512]{2,1,0:T(8,128)(2,1)}, bf16[16,16,512]{2,1,0:T(8,128)(2,1)}, bf16[8,16,512...) custom-call(bf16[3,4096]{1,0:T(4,128)(2,1)} %coords_hbm.1, f32[16,4096]{1,0:T(8,128)} %vectors_hbm.1, ...), custom_call_target="tpu_custom_call" | custom-call | tf_op jit(solution)/shard_map/pallas_call | solution.py:414
  38.4 15.4 %shard_map.137 = f32[16,4096]{1,0:T(8,128)} custom-call(s32[8,128]{1,0:T(8,128)} %get-tuple-element.12.pairs, f32[16,4096]{1,0:T(8,128)} %get-tuple-element.13.total_hbm, bf16[8,16,512]{2,1,0:T(8,128)(2,1)} %get-tuple-element.14.own_vec, bf16[16,16,512]{2,1,0:T(8,128)(2,1)} %get-tuple-element.15.side_vec, bf16[8,16,512]{2,1,0:T(8,128)(2,1)} %get-tuple-element.16.own_source, ...), custom_call_target="tpu_custom_call" | custom-call | tf_op jit(solution)/shard_map/pallas_call | solution.py:522

commit v3 on v2

--- a/solution.py
+++ b/solution.py
@@ -30,8 +30,9 @@
 OWN_DONE = OWN_TURNS * TURN
 SIDE_DONE = (MID_TURNS + LAST_TURNS) * TURN
 SCALE = POINTS**-0.5
-VMEM_LIMIT = 63 << 20
+VMEM_LIMIT = 30 << 20
 HBM = pl.BlockSpec(memory_space=pltpu.HBM)
+ANY = pl.BlockSpec(memory_space=pl.ANY)
 VMEM = pl.BlockSpec(memory_space=pltpu.VMEM)
 SMEM = pl.BlockSpec(memory_space=pltpu.SMEM)
 
@@ -125,6 +126,11 @@
     far_three_hbm,
     total,
     pairs,
+    own_vec_out,
+    side_vec_out,
+    own_source_out,
+    side_source_out,
+    target_out,
     own_vec,
     side_vec,
     own_source,
@@ -150,12 +156,15 @@
     raw,
     dist,
     tasks,
+    down_three,
+    down_leaf,
     toward,
     level_two,
     level_three,
     row_one,
     load_sem,
     task_sem,
+    out_sem,
     side_send,
     side_recv,
     toward_send,
@@ -246,6 +255,78 @@
             pos_f32[row : row + 1, :] = coords[comp : comp + 1, span(box)].astype(F32)
     pos_f32[24:32, :] = jnp.zeros((8, POINTS), F32)
     pos[...] = pos_f32[...].astype(BF)
+    def send(ref, sends, recvs, step, slot, peer):
+        return pltpu.make_async_remote_copy(
+            src_ref=ref,
+            dst_ref=ref,
+            send_sem=sends.at[step],
+            recv_sem=recvs.at[slot],
+            device_id=peer,
+            device_id_type=MESH,
+        )
+
+    def toward_copy(step, slot):
+        return send(toward.at[z], toward_send, toward_recv, step, slot, (gx, in_line(step)))
+
+    def line_copy(step, slot):
+        return send(row_one.at[gy], line_send, line_recv, step, slot, (gx, in_line(step)))
+
+    def two_copy(step, slot):
+        return send(level_two.at[x], two_send, two_recv, step, slot, (gx, in_plane(step)))
+
+    def row_copy(step, slot):
+        part = row_one.at[pl.ds(x * LINE, LINE)]
+        return send(part, row_send, row_recv, step, slot, (gx, in_plane(step)))
+
+    def three_copy(step, slot):
+        return send(level_three.at[gx], three_send, three_recv, step, slot, ((gx + step) % GX, gy))
+
+    def each(count, do):
+        def body(n, carry):
+            do(n)
+            return carry
+
+        lax.fori_loop(1, count, body, 0)
+
+    def start_all(copy, mine, count):
+        each(count, lambda n: copy(n, mine).start())
+
+    def start_far_first(copy, mine):
+        for n in (8, 7, 9, 6, 10, 5, 11, 4, 12, 3, 13, 2, 14, 1, 15):
+            copy(n, mine).start()
+
+    def arrive_all(copy, mine, count):
+        each(count, lambda n: copy(n, (mine + n) % count).wait_recv())
+
+    def sent_all(copy, mine, count):
+        each(count, lambda n: copy(n, mine).wait_send())
+
+    sides = []
+    for n, (source, goal, rows) in enumerate(((own_vec, side_vec, 8), (pos, side_pos, 32))):
+        for side, peer in ((0, right), (1, left)):
+            sides.append(
+                pltpu.make_async_remote_copy(
+                    src_ref=source,
+                    dst_ref=goal.at[pl.ds(side * rows, rows)],
+                    send_sem=side_send.at[2 * n + side],
+                    recv_sem=side_recv.at[2 * n + side],
+                    device_id=(gx, peer),
+                    device_id_type=MESH,
+                )
+            )
+
+    def enter():
+        pl.semaphore_wait(barrier, LINE - 1 + LINES - 1 + GX - 1 + 2)
+        start_far_first(toward_copy, z)
+        start_far_first(line_copy, z)
+        for copy in sides:
+            copy.start()
+
+    late = (z // 8) * (1 - z // 12)
+    ahead = (1 - z // 8) * (OWN_TURNS - z // 2) + z // 14
+
+    pl.when(late == 1)(enter)
+
     loads[2].wait()
     loads[3].wait()
     pair_lists(near_list, near_count, gy, gy_count, pairs)
@@ -260,6 +341,20 @@
     target[...] = raw[...].astype(BF)
     set_rows(raw, 0, [-2.0 * part for part in parts] + norms + ones)
     own_source[...] = raw[...].astype(BF)
+    outs = [
+        pltpu.make_async_copy(source, goal, out_sem.at[n])
+        for n, (source, goal) in enumerate(
+            (
+                (own_vec, own_vec_out),
+                (own_source, own_source_out),
+                (target, target_out),
+                (side_vec, side_vec_out),
+                (side_source, side_source_out),
+            )
+        )
+    ]
+    for copy in outs[:3]:
+        copy.start()
     total[...] = jnp.zeros_like(total)
     task_copy.wait()
 
@@ -283,77 +378,19 @@
 
         lax.fori_loop(first, last, turn, 0)
 
-    ahead = (1 - z // 8) * (OWN_TURNS - z // 2) + z // 14
     begin(0, own_source, 0)
     fill(0, own_source, own_vec, 0, ahead)
 
-    pl.semaphore_wait(barrier, LINE - 1 + LINES - 1 + GX - 1 + 2)
-
-    def send(ref, sends, recvs, step, slot, peer):
-        return pltpu.make_async_remote_copy(
-            src_ref=ref,
-            dst_ref=ref,
-            send_sem=sends.at[step],
-            recv_sem=recvs.at[slot],
-            device_id=peer,
-            device_id_type=MESH,
-        )
-
-    def toward_copy(step, slot):
-        return send(toward.at[z], toward_send, toward_recv, step, slot, (gx, in_line(step)))
-
-    def line_copy(step, slot):
-        return send(row_one.at[gy], line_send, line_recv, step, slot, (gx, in_line(step)))
-
-    def two_copy(step, slot):
-        return send(level_two.at[x], two_send, two_recv, step, slot, (gx, in_plane(step)))
-
-    def row_copy(step, slot):
-        part = row_one.at[pl.ds(x * LINE, LINE)]
-        return send(part, row_send, row_recv, step, slot, (gx, in_plane(step)))
-
-    def three_copy(step, slot):
-        return send(level_three.at[gx], three_send, three_recv, step, slot, ((gx + step) % GX, gy))
-
-    def each(count, do):
-        def body(n, carry):
-            do(n)
-            return carry
-
-        lax.fori_loop(1, count, body, 0)
-
-    def start_all(copy, mine, count):
-        each(count, lambda n: copy(n, mine).start())
-
-    def start_far_first(copy, mine):
-        for n in (8, 7, 9, 6, 10, 5, 11, 4, 12, 3, 13, 2, 14, 1, 15):
-            copy(n, mine).start()
-
-    def arrive_all(copy, mine, count):
-        each(count, lambda n: copy(n, (mine + n) % count).wait_recv())
-
-    def sent_all(copy, mine, count):
-        each(count, lambda n: copy(n, mine).wait_send())
-
-    start_far_first(toward_copy, z)
-    sides = []
-    for n, (source, goal, rows) in enumerate(((own_vec, side_vec, 8), (pos, side_pos, 32))):
-        for side, peer in ((0, right), (1, left)):
-            sides.append(
-                pltpu.make_async_remote_copy(
-                    src_ref=source,
-                    dst_ref=goal.at[pl.ds(side * rows, rows)],
-                    send_sem=side_send.at[2 * n + side],
-                    recv_sem=side_recv.at[2 * n + side],
-                    device_id=(gx, peer),
-                    device_id_type=MESH,
-                )
-            )
-    for copy in sides:
-        copy.start()
-    start_far_first(line_copy, z)
+    pl.when(late == 0)(enter)
 
     fill(0, own_source, own_vec, ahead, OWN_TURNS)
+
+    for load in loads[7:]:
+        load.wait()
+    down = dot(mid_up[0], top_up[group]).astype(BF)
+    down_three[...] = dot_t(couple_three[0].reshape(FAR * RANK, RANK), down).astype(BF)
+    for b in range(BOXES):
+        down_leaf[b * POINTS : (b + 1) * POINTS, :] = dot(basis[b], leaf_up[b]).astype(BF)
 
     arrive_all(toward_copy, z, LINE)
     for half in range(2):
@@ -373,31 +410,31 @@
         parts = [near[n * BOXES : (n + 1) * BOXES, :] for n in range(3)]
         set_rows(raw, 0, [-2.0 * part for part in parts] + norm_parts(parts))
         side_source[side * BOXES : (side + 1) * BOXES] = raw[...].astype(BF)
+    for copy in outs[3:]:
+        copy.start()
     begin(3, side_source, 0)
     fill(3, side_source, side_vec, 0, MID_TURNS)
 
-    loads[7].wait()
     arrive_all(two_copy, x, LINES)
     twos = jnp.concatenate([level_two[n // 2, n % 2] for n in range(8)], axis=1)
     level_three[gx] = dot(twos, top_up[...].reshape(8 * RANK, RANK)).astype(BF)
     start_all(three_copy, gx, GX)
 
-    for load in loads[8:]:
-        load.wait()
     source_two = gather(level_two, lambda f: (far_two[group, f] // 2, far_two[group, f] % 2))
     local_two = dot(source_two, couple_two[...].reshape(FAR * RANK, RANK))
+    local_one = dot_t(local_two.astype(BF), mid_up[0])
+    fill(3, side_source, side_vec, MID_TURNS, MID_TURNS + LAST_TURNS)
+
     arrive_all(row_copy, x, LINES)
-    local_one = dot(gather(row_one, lambda f: far_one[0, f]), couple_one[0].reshape(FAR * RANK, RANK))
-    fill(3, side_source, side_vec, MID_TURNS, MID_TURNS + LAST_TURNS)
-
+    local_one = local_one + dot(
+        gather(row_one, lambda f: far_one[0, f]), couple_one[0].reshape(FAR * RANK, RANK)
+    )
     arrive_all(three_copy, gx, GX)
-    local_three = dot(gather(level_three, lambda f: far_three[0, f]), couple_three[0].reshape(FAR * RANK, RANK))
-    local_two = local_two + dot_t(local_three.astype(BF), top_up[group])
-    local_one = local_one + dot_t(local_two.astype(BF), mid_up[0])
-    local_leaf = dot_t(local_one.astype(BF), ups).astype(BF)
-    for b in range(BOXES):
-        total[:, span(b)] += dot_t(local_leaf[:, b * RANK : (b + 1) * RANK], basis[b])
-
+    local_one = local_one + dot(gather(level_three, lambda f: far_three[0, f]), down_three[...])
+    total[...] += dot_t(local_one.astype(BF), down_leaf[...])
+
+    for copy in outs:
+        copy.wait()
     for copy in sides:
         copy.wait_send()
     sent_all(toward_copy, z, LINE)
@@ -423,8 +460,13 @@
             jax.ShapeDtypeStruct(boxes, BF),
         ),
         in_specs=[HBM] * 14,
-        out_specs=(VMEM,) * 7,
+        out_specs=(VMEM, VMEM) + (ANY,) * 5,
         scratch_shapes=[
+            pltpu.VMEM(boxes, BF),
+            pltpu.VMEM(sides, BF),
+            pltpu.VMEM(boxes, BF),
+            pltpu.VMEM(sides, BF),
+            pltpu.VMEM(boxes, BF),
             pltpu.VMEM((3, WIDTH), BF),
             pltpu.VMEM((PROBES, WIDTH), F32),
             pltpu.VMEM((BOXES, NEAR), I32),
@@ -445,12 +487,15 @@
             pltpu.VMEM(boxes, F32),
             pltpu.VMEM((2, POINTS, POINTS), F32),
             pltpu.SMEM((8, 128), I32),
+            pltpu.VMEM((FAR * RANK, RANK), BF),
+            pltpu.VMEM((WIDTH, RANK), BF),
             pltpu.VMEM((LINE, PROBES, RANK), BF),
             pltpu.VMEM((LINES, 2, PROBES, RANK), BF),
             pltpu.VMEM((GX, PROBES, RANK), BF),
             pltpu.VMEM((LINE * LINES, PROBES, RANK), BF),
             dma((14,)),
             dma((1,)),
+            dma((5,)),
             dma((4,)),
             dma((4,)),
             dma((LINE,)),
@@ -470,11 +515,12 @@
     )(*arrays)
 
 
-def near_kernel(pairs, total_hbm, own_vec, side_vec, own_source, side_source, target_hbm, out, vec, source, target, dist, sem):
+def near_kernel(pairs_hbm, total_hbm, own_vec, side_vec, own_source, side_source, target_hbm, out, pairs, vec, source, target, dist, sem):
     loads = [
         pltpu.make_async_copy(a, b, sem.at[n])
         for n, (a, b) in enumerate(
             (
+                (pairs_hbm, pairs),
                 (own_source, source.at[pl.ds(0, BOXES)]),
                 (side_source, source.at[pl.ds(BOXES, 2 * BOXES)]),
                 (target_hbm, target),
@@ -486,6 +532,7 @@
     ]
     for load in loads:
         load.start()
+    loads[0].wait()
     own = jnp.maximum(pairs[6, 0] - OWN_DONE, 0)
     tasks = own + jnp.maximum(pairs[7, 0] - SIDE_DONE, 0)
 
@@ -496,7 +543,7 @@
         place = pairs[row + 1, lane] + jnp.where(mine, 0, BOXES)
         return pairs[row, lane], place, jnp.where(task < tasks, pairs[row + 2, lane], 0)
 
-    for load in loads:
+    for load in loads[1:]:
         load.wait()
 
     def measure(task):
@@ -522,14 +569,15 @@
     return pl.pallas_call(
         near_kernel,
         out_shape=jax.ShapeDtypeStruct((PROBES, WIDTH), F32),
-        in_specs=[SMEM] + [HBM] * 6,
+        in_specs=[ANY] * 7,
         out_specs=VMEM,
         scratch_shapes=[
+            pltpu.SMEM((8, 128), I32),
             pltpu.VMEM((3 * BOXES, PROBES, POINTS), BF),
             pltpu.VMEM((3 * BOXES, PROBES, POINTS), BF),
             pltpu.VMEM((BOXES, PROBES, POINTS), BF),
             pltpu.VMEM((2, POINTS, POINTS), F32),
-            pltpu.SemaphoreType.DMA((6,)),
+            pltpu.SemaphoreType.DMA((7,)),
         ],
         compiler_params=pltpu.CompilerParams(vmem_limit_bytes=VMEM_LIMIT),
     )(pairs, total, *arrays)
@@ -537,7 +585,8 @@
 
 def local(gy_count, coords, vectors, *rest):
     matrices, near_list, near_count = rest[:-2], rest[-2], rest[-1]
-    return near_field(*far_field(gy_count, coords, vectors, near_list, near_count, *matrices))
+    arrays = (coords, vectors, near_list, near_count, *matrices)
+    return near_field(*far_field(gy_count, *(pltpu.with_memory_space_constraint(a, pltpu.HBM) for a in arrays)))
 
 
 def solution(mesh):

time: 53.9 us -> 46.9 us (0.87)
  the two profiles are of different devices: /device:TPU:64 before, /device:TPU:90 now
where the time goes in v3:
time: 46.9 us; the launch traced here: 46.8 us
  Pallas kernels  46.8 us (100%)
    pallas_call x1, Pallas kernels, far_field(): pl.pallas_call(functools.partial(far_kernel, gy_count), out_shape=(jax.Sh...  32.8 us
    pallas_call x1, Pallas kernels, near_field(): pl.pallas_call(near_kernel, out_shape=jax.ShapeDtypeStruct((PROBES, WIDTH...  14 us

profile of v3, /device:TPU:90, one launch (start us, length us, event | category | flops | bytes accessed | tf_op | source)
XLA Modules:
  0.0 46.8 jit_solution(5905819143385177116)
XLA Ops:
  0.0 32.8 %shard_map.136 = (f32[16,4096]{1,0:T(8,128)S(1)}, s32[8,128]{1,0:T(8,128)S(1)}, bf16[8,16,512]{2,1,0:T(8,128)(2,1)S(1)}, bf16[16,16,512]{2,1,0:T(8,128)(2,1)S(1)...) custom-call(bf16[3,4096]{1,0:T(4,128)(2,1)} %coords_hbm.1, ...), custom_call_target="tpu_custom_call" | custom-call | tf_op jit(solution)/shard_map/pallas_call | solution.py:451
  32.8 14.0 %shard_map.137 = f32[16,4096]{1,0:T(8,128)} custom-call(s32[8,128]{1,0:T(8,128)S(1)} %get-tuple-element.12.pairs_hbm, f32[16,4096]{1,0:T(8,128)S(1)} %get-tuple-element.13.total_hbm, bf16[8,16,512]{2,1,0:T(8,128)(2,1)S(1)} %get-tuple-element.14.own_vec, bf16[16,16,512]{2,1,0:T(8,128)(2,1)S(1)} %get-tuple-element.15.side_vec, ...), custom_call_target="tpu_custom_call" | custom-call | tf_op jit(solution)/shard_map/pallas_call | solution.py:569

commit v4 on v3

--- a/solution.py
+++ b/solution.py
@@ -23,10 +23,10 @@
 LINE = 16
 LINES = 4
 GROUP = 8
-TURN = 4
-OWN_TURNS = 7
-MID_TURNS = 2
-LAST_TURNS = 2
+TURN = 6
+OWN_TURNS = 5
+MID_TURNS = 1
+LAST_TURNS = 3
 OWN_DONE = OWN_TURNS * TURN
 SIDE_DONE = (MID_TURNS + LAST_TURNS) * TURN
 SCALE = POINTS**-0.5
@@ -204,8 +204,8 @@
             )
         )
     ]
-    for load in loads:
-        load.start()
+    for n in (0, 1, 4, 5, 6):
+        loads[n].start()
 
     right = (gy + 1) % gy_count
     left = (gy + gy_count - 1) % gy_count
@@ -235,6 +235,16 @@
     lax.fori_loop(1, GX, greet_three, 0)
     greet((gx, left))
     greet((gx, right))
+    for n in (2, 3, *range(7, 14)):
+        loads[n].start()
+
+    loads[1].wait()
+    for comp in range(3):
+        for box in range(BOXES):
+            row = comp * BOXES + box
+            pos_f32[row : row + 1, :] = coords[comp : comp + 1, span(box)].astype(F32)
+    pos_f32[24:32, :] = jnp.zeros((8, POINTS), F32)
+    pos[...] = pos_f32[...].astype(BF)
 
     loads[0].wait()
     for box in range(BOXES):
@@ -248,13 +258,6 @@
     loads[6].wait()
     toward[z] = dot(one, mid_up[0]).astype(BF)
 
-    loads[1].wait()
-    for comp in range(3):
-        for box in range(BOXES):
-            row = comp * BOXES + box
-            pos_f32[row : row + 1, :] = coords[comp : comp + 1, span(box)].astype(F32)
-    pos_f32[24:32, :] = jnp.zeros((8, POINTS), F32)
-    pos[...] = pos_f32[...].astype(BF)
     def send(ref, sends, recvs, step, slot, peer):
         return pltpu.make_async_remote_copy(
             src_ref=ref,
@@ -318,20 +321,14 @@
     def enter():
         pl.semaphore_wait(barrier, LINE - 1 + LINES - 1 + GX - 1 + 2)
         start_far_first(toward_copy, z)
-        start_far_first(line_copy, z)
         for copy in sides:
             copy.start()
+        start_far_first(line_copy, z)
 
     late = (z // 8) * (1 - z // 12)
-    ahead = (1 - z // 8) * (OWN_TURNS - z // 2) + z // 14
+    ahead = (1 - z // 8) * (OWN_TURNS - (z // 4) * (z // 2 - 1)) + z // 12
 
     pl.when(late == 1)(enter)
-
-    loads[2].wait()
-    loads[3].wait()
-    pair_lists(near_list, near_count, gy, gy_count, pairs)
-    task_copy = pltpu.make_async_copy(pairs, tasks, task_sem.at[0])
-    task_copy.start()
 
     raw[...] = jnp.zeros_like(raw)
     ones = [jnp.ones((BOXES, POINTS), F32)] * 3
@@ -356,6 +353,12 @@
     for copy in outs[:3]:
         copy.start()
     total[...] = jnp.zeros_like(total)
+    loads[2].wait()
+    loads[3].wait()
+    pair_lists(near_list, near_count, gy, gy_count, pairs)
+    task_copy = pltpu.make_async_copy(pairs, tasks, task_sem.at[0])
+    task_copy.start()
+
     task_copy.wait()
 
     def begin(first_row, source_ref, task):
@@ -399,9 +402,6 @@
             two = two + toward[half * GROUP + n].astype(F32)
         level_two[x, half] = two.astype(BF)
     start_all(two_copy, x, LINES)
-    arrive_all(line_copy, z, LINE)
-    start_all(row_copy, x, LINES)
-
     for copy in sides:
         copy.wait_recv()
     for side in range(2):
@@ -419,18 +419,20 @@
     twos = jnp.concatenate([level_two[n // 2, n % 2] for n in range(8)], axis=1)
     level_three[gx] = dot(twos, top_up[...].reshape(8 * RANK, RANK)).astype(BF)
     start_all(three_copy, gx, GX)
+    arrive_all(line_copy, z, LINE)
+    start_all(row_copy, x, LINES)
 
     source_two = gather(level_two, lambda f: (far_two[group, f] // 2, far_two[group, f] % 2))
     local_two = dot(source_two, couple_two[...].reshape(FAR * RANK, RANK))
     local_one = dot_t(local_two.astype(BF), mid_up[0])
     fill(3, side_source, side_vec, MID_TURNS, MID_TURNS + LAST_TURNS)
 
+    arrive_all(three_copy, gx, GX)
+    local_one = local_one + dot(gather(level_three, lambda f: far_three[0, f]), down_three[...])
     arrive_all(row_copy, x, LINES)
     local_one = local_one + dot(
         gather(row_one, lambda f: far_one[0, f]), couple_one[0].reshape(FAR * RANK, RANK)
     )
-    arrive_all(three_copy, gx, GX)
-    local_one = local_one + dot(gather(level_three, lambda f: far_three[0, f]), down_three[...])
     total[...] += dot_t(local_one.astype(BF), down_leaf[...])
 
     for copy in outs:
@@ -515,69 +517,59 @@
     )(*arrays)
 
 
-def near_kernel(pairs_hbm, total_hbm, own_vec, side_vec, own_source, side_source, target_hbm, out, pairs, vec, source, target, dist, sem):
-    loads = [
-        pltpu.make_async_copy(a, b, sem.at[n])
-        for n, (a, b) in enumerate(
-            (
-                (pairs_hbm, pairs),
-                (own_source, source.at[pl.ds(0, BOXES)]),
-                (side_source, source.at[pl.ds(BOXES, 2 * BOXES)]),
-                (target_hbm, target),
-                (own_vec, vec.at[pl.ds(0, BOXES)]),
-                (side_vec, vec.at[pl.ds(BOXES, 2 * BOXES)]),
-                (total_hbm, out),
-            )
-        )
-    ]
-    for load in loads:
-        load.start()
-    loads[0].wait()
+def near_kernel(pairs_hbm, total, own_vec, side_vec, own_source, side_source, target, out, pairs, dist, sem):
+    load = pltpu.make_async_copy(pairs_hbm, pairs, sem.at[0])
+    load.start()
+    out[...] = total[...]
+    load.wait()
     own = jnp.maximum(pairs[6, 0] - OWN_DONE, 0)
-    tasks = own + jnp.maximum(pairs[7, 0] - SIDE_DONE, 0)
-
-    def find(task):
-        mine = task < own
-        row = jnp.where(mine, 0, 3)
-        lane = jnp.minimum(jnp.where(mine, OWN_DONE + task, SIDE_DONE + task - own), 127)
-        place = pairs[row + 1, lane] + jnp.where(mine, 0, BOXES)
-        return pairs[row, lane], place, jnp.where(task < tasks, pairs[row + 2, lane], 0)
-
-    for load in loads[1:]:
-        load.wait()
-
-    def measure(task):
-        box, place, _ = find(task)
-        return squares(source[place], target[box])
-
-    dist[0] = measure(0)
-
-    def turn(n, carry):
-        for k in range(TURN):
-            task = n * TURN + k
-            square = dist[k % 2]
-            dist[1 - k % 2] = measure(task + 1)
-            box, place, times = find(task)
-            lanes = pl.ds(pl.multiple_of(box * POINTS, POINTS), POINTS)
-            out[:, lanes] += (times.astype(F32) * SCALE) * dot(vec[place], tile_of(square))
+    side = jnp.maximum(pairs[7, 0] - SIDE_DONE, 0)
+
+    def measure(row, source, task):
+        lane = jnp.minimum(task, 127)
+        return squares(source[pairs[row + 1, lane]], target[pairs[row, lane]])
+
+    def add(row, vec, task, square):
+        lanes = pl.ds(pl.multiple_of(pairs[row, task] * POINTS, POINTS), POINTS)
+        weight = pairs[row + 2, task].astype(F32) * SCALE
+        out[:, lanes] += weight * dot(vec[pairs[row + 1, task]], tile_of(square))
+
+    def single(n, carry):
+        add(0, own_vec, OWN_DONE + n, measure(0, own_source, OWN_DONE + n))
         return carry
 
-    lax.fori_loop(0, (tasks + TURN - 1) // TURN, turn, 0)
+    lax.fori_loop(0, own, single, 0)
+
+    dist[0] = measure(3, side_source, SIDE_DONE)
+
+    def turns(width, first):
+        def turn(n, carry):
+            for k in range(width):
+                task = first + n * width + k
+                square = dist[k % 2]
+                dist[1 - k % 2] = measure(3, side_source, task + 1)
+                add(3, side_vec, task, square)
+            return carry
+
+        return turn
+
+    whole = side // TURN
+    rest = side % TURN
+    lax.fori_loop(0, whole, turns(TURN, SIDE_DONE), 0)
+    lax.fori_loop(0, rest // 2, turns(2, SIDE_DONE + whole * TURN), 0)
+    lax.fori_loop(0, rest % 2, turns(1, SIDE_DONE + side - 1), 0)
 
 
 def near_field(total, pairs, *arrays):
     return pl.pallas_call(
         near_kernel,
         out_shape=jax.ShapeDtypeStruct((PROBES, WIDTH), F32),
-        in_specs=[ANY] * 7,
+        in_specs=[ANY] + [VMEM] * 6,
         out_specs=VMEM,
         scratch_shapes=[
             pltpu.SMEM((8, 128), I32),
-            pltpu.VMEM((3 * BOXES, PROBES, POINTS), BF),
-            pltpu.VMEM((3 * BOXES, PROBES, POINTS), BF),
-            pltpu.VMEM((BOXES, PROBES, POINTS), BF),
             pltpu.VMEM((2, POINTS, POINTS), F32),
-            pltpu.SemaphoreType.DMA((7,)),
+            pltpu.SemaphoreType.DMA((1,)),
         ],
         compiler_params=pltpu.CompilerParams(vmem_limit_bytes=VMEM_LIMIT),
     )(pairs, total, *arrays)

time: 46.9 us -> 46.8 us (level)
  the two profiles are of different devices: /device:TPU:90 before, /device:TPU:18 now
where the time goes in v4:
time: 46.8 us; the launch traced here: 46.7 us
  Pallas kernels  46.5 us (99%)
    pallas_call x1, Pallas kernels, far_field(): pl.pallas_call(functools.partial(far_kernel, gy_count), out_shape=(jax.Sh...  38 us
    pallas_call x1, Pallas kernels, near_field(): pl.pallas_call(near_kernel, out_shape=jax.ShapeDtypeStruct((PROBES, WIDTH...  8.54 us

profile of v4, /device:TPU:18, one launch (start us, length us, event | category | flops | bytes accessed | tf_op | source)
XLA Modules:
  0.0 46.7 jit_solution(1818080364917121986)
XLA Ops:
  0.0 38.0 %shard_map.136 = (f32[16,4096]{1,0:T(8,128)S(1)}, s32[8,128]{1,0:T(8,128)S(1)}, bf16[8,16,512]{2,1,0:T(8,128)(2,1)S(1)}, bf16[16,16,512]{2,1,0:T(8,128)(2,1)S(1)...) custom-call(bf16[3,4096]{1,0:T(4,128)(2,1)} %coords_hbm.1, ...), custom_call_target="tpu_custom_call" | custom-call | tf_op jit(solution)/shard_map/pallas_call | solution.py:453
  38.0 8.5 %shard_map.137 = f32[16,4096]{1,0:T(8,128)} custom-call(s32[8,128]{1,0:T(8,128)S(1)} %get-tuple-element.12.pairs_hbm, f32[16,4096]{1,0:T(8,128)S(1)} %get-tuple-element.13.total, bf16[8,16,512]{2,1,0:T(8,128)(2,1)S(1)} %get-tuple-element.14.own_vec, bf16[16,16,512]{2,1,0:T(8,128)(2,1)S(1)} %get-tuple-element.15.side_vec, ...), custom_call_target="tpu_custom_call" | custom-call | tf_op jit(solution)/shard_map/pallas_call | solution.py:564

commit v5 on v4

--- a/solution.py
+++ b/solution.py
@@ -167,16 +167,11 @@
     out_sem,
     side_send,
     side_recv,
-    toward_send,
-    toward_recv,
-    line_send,
-    line_recv,
-    two_send,
-    two_recv,
-    row_send,
-    row_recv,
-    three_send,
-    three_recv,
+    toward_sem,
+    line_sem,
+    two_sem,
+    row_sem,
+    three_sem,
 ):
     gx = lax.axis_index("gx")
     gy = lax.axis_index("gy")
@@ -258,51 +253,34 @@
     loads[6].wait()
     toward[z] = dot(one, mid_up[0]).astype(BF)
 
-    def send(ref, sends, recvs, step, slot, peer):
+    def copy(ref, sems, peer):
         return pltpu.make_async_remote_copy(
             src_ref=ref,
             dst_ref=ref,
-            send_sem=sends.at[step],
-            recv_sem=recvs.at[slot],
+            send_sem=sems.at[0],
+            recv_sem=sems.at[1],
             device_id=peer,
             device_id_type=MESH,
         )
 
-    def toward_copy(step, slot):
-        return send(toward.at[z], toward_send, toward_recv, step, slot, (gx, in_line(step)))
-
-    def line_copy(step, slot):
-        return send(row_one.at[gy], line_send, line_recv, step, slot, (gx, in_line(step)))
-
-    def two_copy(step, slot):
-        return send(level_two.at[x], two_send, two_recv, step, slot, (gx, in_plane(step)))
-
-    def row_copy(step, slot):
-        part = row_one.at[pl.ds(x * LINE, LINE)]
-        return send(part, row_send, row_recv, step, slot, (gx, in_plane(step)))
-
-    def three_copy(step, slot):
-        return send(level_three.at[gx], three_send, three_recv, step, slot, ((gx + step) % GX, gy))
-
-    def each(count, do):
-        def body(n, carry):
-            do(n)
-            return carry
-
-        lax.fori_loop(1, count, body, 0)
-
-    def start_all(copy, mine, count):
-        each(count, lambda n: copy(n, mine).start())
-
-    def start_far_first(copy, mine):
+    def start_far_first(ref, sems):
         for n in (8, 7, 9, 6, 10, 5, 11, 4, 12, 3, 13, 2, 14, 1, 15):
-            copy(n, mine).start()
-
-    def arrive_all(copy, mine, count):
-        each(count, lambda n: copy(n, (mine + n) % count).wait_recv())
-
-    def sent_all(copy, mine, count):
-        each(count, lambda n: copy(n, mine).wait_send())
+            copy(ref, sems, (gx, in_line(n))).start()
+
+    def start_plane(ref, sems):
+        for n in (2, 1, 3):
+            copy(ref, sems, (gx, in_plane(n))).start()
+
+    def start_three(ref, sems):
+        for n in (4, 5, 3, 2, 6, 7, 1):
+            copy(ref, sems, ((gx + n) % GX, gy)).start()
+
+    line_peer, plane_peer, three_peer = (gx, in_line(1)), (gx, in_plane(1)), ((gx + 1) % GX, gy)
+    all_toward = copy(toward.at[pl.ds(0, LINE - 1)], toward_sem, line_peer)
+    all_lines = copy(row_one.at[pl.ds(0, LINE - 1)], line_sem, line_peer)
+    all_two = copy(level_two.at[pl.ds(0, LINES - 1)], two_sem, plane_peer)
+    all_rows = copy(row_one.at[pl.ds(0, (LINES - 1) * LINE)], row_sem, plane_peer)
+    all_three = copy(level_three.at[pl.ds(0, GX - 1)], three_sem, three_peer)
 
     sides = []
     for n, (source, goal, rows) in enumerate(((own_vec, side_vec, 8), (pos, side_pos, 32))):
@@ -318,17 +296,20 @@
                 )
             )
 
-    def enter():
+    def enter(rows_first):
         pl.semaphore_wait(barrier, LINE - 1 + LINES - 1 + GX - 1 + 2)
-        start_far_first(toward_copy, z)
-        for copy in sides:
-            copy.start()
-        start_far_first(line_copy, z)
+        start_far_first(toward.at[z], toward_sem)
+        if rows_first:
+            start_far_first(row_one.at[gy], line_sem)
+        for side_copy in sides:
+            side_copy.start()
+        if not rows_first:
+            start_far_first(row_one.at[gy], line_sem)
 
     late = (z // 8) * (1 - z // 12)
     ahead = (1 - z // 8) * (OWN_TURNS - (z // 4) * (z // 2 - 1)) + z // 12
 
-    pl.when(late == 1)(enter)
+    pl.when(late == 1)(functools.partial(enter, True))
 
     raw[...] = jnp.zeros_like(raw)
     ones = [jnp.ones((BOXES, POINTS), F32)] * 3
@@ -350,8 +331,8 @@
             )
         )
     ]
-    for copy in outs[:3]:
-        copy.start()
+    for out_copy in outs[:3]:
+        out_copy.start()
     total[...] = jnp.zeros_like(total)
     loads[2].wait()
     loads[3].wait()
@@ -384,7 +365,7 @@
     begin(0, own_source, 0)
     fill(0, own_source, own_vec, 0, ahead)
 
-    pl.when(late == 0)(enter)
+    pl.when(late == 0)(functools.partial(enter, False))
 
     fill(0, own_source, own_vec, ahead, OWN_TURNS)
 
@@ -395,55 +376,52 @@
     for b in range(BOXES):
         down_leaf[b * POINTS : (b + 1) * POINTS, :] = dot(basis[b], leaf_up[b]).astype(BF)
 
-    arrive_all(toward_copy, z, LINE)
+    all_toward.wait_recv()
     for half in range(2):
         two = jnp.zeros((PROBES, RANK), F32)
         for n in range(GROUP):
             two = two + toward[half * GROUP + n].astype(F32)
         level_two[x, half] = two.astype(BF)
-    start_all(two_copy, x, LINES)
-    for copy in sides:
-        copy.wait_recv()
+    start_plane(level_two.at[x], two_sem)
+    for side_copy in sides:
+        side_copy.wait_recv()
     for side in range(2):
         first = side * 32
         near = side_pos[first : first + 24, :].astype(F32)
         parts = [near[n * BOXES : (n + 1) * BOXES, :] for n in range(3)]
         set_rows(raw, 0, [-2.0 * part for part in parts] + norm_parts(parts))
         side_source[side * BOXES : (side + 1) * BOXES] = raw[...].astype(BF)
-    for copy in outs[3:]:
-        copy.start()
+    for out_copy in outs[3:]:
+        out_copy.start()
     begin(3, side_source, 0)
     fill(3, side_source, side_vec, 0, MID_TURNS)
 
-    arrive_all(two_copy, x, LINES)
+    all_two.wait_recv()
     twos = jnp.concatenate([level_two[n // 2, n % 2] for n in range(8)], axis=1)
     level_three[gx] = dot(twos, top_up[...].reshape(8 * RANK, RANK)).astype(BF)
-    start_all(three_copy, gx, GX)
-    arrive_all(line_copy, z, LINE)
-    start_all(row_copy, x, LINES)
+    start_three(level_three.at[gx], three_sem)
+    all_lines.wait_recv()
+    start_plane(row_one.at[pl.ds(x * LINE, LINE)], row_sem)
 
     source_two = gather(level_two, lambda f: (far_two[group, f] // 2, far_two[group, f] % 2))
     local_two = dot(source_two, couple_two[...].reshape(FAR * RANK, RANK))
     local_one = dot_t(local_two.astype(BF), mid_up[0])
     fill(3, side_source, side_vec, MID_TURNS, MID_TURNS + LAST_TURNS)
 
-    arrive_all(three_copy, gx, GX)
+    all_three.wait_recv()
     local_one = local_one + dot(gather(level_three, lambda f: far_three[0, f]), down_three[...])
-    arrive_all(row_copy, x, LINES)
+    all_rows.wait_recv()
     local_one = local_one + dot(
         gather(row_one, lambda f: far_one[0, f]), couple_one[0].reshape(FAR * RANK, RANK)
     )
     total[...] += dot_t(local_one.astype(BF), down_leaf[...])
 
-    for copy in outs:
-        copy.wait()
-    for copy in sides:
-        copy.wait_send()
-    sent_all(toward_copy, z, LINE)
-    sent_all(line_copy, z, LINE)
-    sent_all(two_copy, x, LINES)
-    sent_all(row_copy, x, LINES)
-    sent_all(three_copy, gx, GX)
+    for out_copy in outs:
+        out_copy.wait()
+    for side_copy in sides:
+        side_copy.wait_send()
+    for exchange in (all_toward, all_lines, all_two, all_rows, all_three):
+        exchange.wait_send()
 
 
 def far_field(gy_count, *arrays):
@@ -500,16 +478,11 @@
             dma((5,)),
             dma((4,)),
             dma((4,)),
-            dma((LINE,)),
-            dma((LINE,)),
-            dma((LINE,)),
-            dma((LINE,)),
-            dma((LINES,)),
-            dma((LINES,)),
-            dma((LINES,)),
-            dma((LINES,)),
-            dma((GX,)),
-            dma((GX,)),
+            dma((2,)),
+            dma((2,)),
+            dma((2,)),
+            dma((2,)),
+            dma((2,)),
         ],
         compiler_params=pltpu.CompilerParams(
             collective_id=0, has_side_effects=True, vmem_limit_bytes=VMEM_LIMIT

time: 46.8 us -> 44.2 us (0.944)
  the two profiles are of different devices: /device:TPU:18 before, /device:TPU:69 now
where the time goes in v5:
time: 44.2 us; the launch traced here: 44.1 us
  Pallas kernels  43.9 us (99%)
    pallas_call x1, Pallas kernels, far_field(): pl.pallas_call(functools.partial(far_kernel, gy_count), out_shape=(jax.Sh...  33.4 us
    pallas_call x1, Pallas kernels, near_field(): pl.pallas_call(near_kernel, out_shape=jax.ShapeDtypeStruct((PROBES, WIDTH...  10.5 us

profile of v5, /device:TPU:69, one launch (start us, length us, event | category | flops | bytes accessed | tf_op | source)
XLA Modules:
  0.0 44.1 jit_solution(8933040996481004927)
XLA Ops:
  0.0 33.4 %shard_map.136 = (f32[16,4096]{1,0:T(8,128)S(1)}, s32[8,128]{1,0:T(8,128)S(1)}, bf16[8,16,512]{2,1,0:T(8,128)(2,1)S(1)}, bf16[16,16,512]{2,1,0:T(8,128)(2,1)S(1)...) custom-call(bf16[3,4096]{1,0:T(4,128)(2,1)} %coords_hbm.1, ...), custom_call_target="tpu_custom_call" | custom-call | tf_op jit(solution)/shard_map/pallas_call | solution.py:431
  33.4 10.5 %shard_map.137 = f32[16,4096]{1,0:T(8,128)} custom-call(s32[8,128]{1,0:T(8,128)S(1)} %get-tuple-element.12.pairs_hbm, f32[16,4096]{1,0:T(8,128)S(1)} %get-tuple-element.13.total, bf16[8,16,512]{2,1,0:T(8,128)(2,1)S(1)} %get-tuple-element.14.own_vec, bf16[16,16,512]{2,1,0:T(8,128)(2,1)S(1)} %get-tuple-element.15.side_vec, ...), custom_call_target="tpu_custom_call" | custom-call | tf_op jit(solution)/shard_map/pallas_call | solution.py:537

commit v6 on v5

--- a/solution.py
+++ b/solution.py
@@ -126,11 +126,6 @@
     far_three_hbm,
     total,
     pairs,
-    own_vec_out,
-    side_vec_out,
-    own_source_out,
-    side_source_out,
-    target_out,
     own_vec,
     side_vec,
     own_source,
@@ -164,7 +159,6 @@
     row_one,
     load_sem,
     task_sem,
-    out_sem,
     side_send,
     side_recv,
     toward_sem,
@@ -319,20 +313,6 @@
     target[...] = raw[...].astype(BF)
     set_rows(raw, 0, [-2.0 * part for part in parts] + norms + ones)
     own_source[...] = raw[...].astype(BF)
-    outs = [
-        pltpu.make_async_copy(source, goal, out_sem.at[n])
-        for n, (source, goal) in enumerate(
-            (
-                (own_vec, own_vec_out),
-                (own_source, own_source_out),
-                (target, target_out),
-                (side_vec, side_vec_out),
-                (side_source, side_source_out),
-            )
-        )
-    ]
-    for out_copy in outs[:3]:
-        out_copy.start()
     total[...] = jnp.zeros_like(total)
     loads[2].wait()
     loads[3].wait()
@@ -391,8 +371,6 @@
         parts = [near[n * BOXES : (n + 1) * BOXES, :] for n in range(3)]
         set_rows(raw, 0, [-2.0 * part for part in parts] + norm_parts(parts))
         side_source[side * BOXES : (side + 1) * BOXES] = raw[...].astype(BF)
-    for out_copy in outs[3:]:
-        out_copy.start()
     begin(3, side_source, 0)
     fill(3, side_source, side_vec, 0, MID_TURNS)
 
@@ -416,8 +394,6 @@
     )
     total[...] += dot_t(local_one.astype(BF), down_leaf[...])
 
-    for out_copy in outs:
-        out_copy.wait()
     for side_copy in sides:
         side_copy.wait_send()
     for exchange in (all_toward, all_lines, all_two, all_rows, all_three):
@@ -440,13 +416,8 @@
             jax.ShapeDtypeStruct(boxes, BF),
         ),
         in_specs=[HBM] * 14,
-        out_specs=(VMEM, VMEM) + (ANY,) * 5,
+        out_specs=(VMEM,) * 7,
         scratch_shapes=[
-            pltpu.VMEM(boxes, BF),
-            pltpu.VMEM(sides, BF),
-            pltpu.VMEM(boxes, BF),
-            pltpu.VMEM(sides, BF),
-            pltpu.VMEM(boxes, BF),
             pltpu.VMEM((3, WIDTH), BF),
             pltpu.VMEM((PROBES, WIDTH), F32),
             pltpu.VMEM((BOXES, NEAR), I32),
@@ -475,7 +446,6 @@
             pltpu.VMEM((LINE * LINES, PROBES, RANK), BF),
             dma((14,)),
             dma((1,)),
-            dma((5,)),
             dma((4,)),
             dma((4,)),
             dma((2,)),

time: 44.2 us -> 44.7 us (1.011)
  the two profiles are of different devices: /device:TPU:69 before, /device:TPU:6 now
where the time goes in v6:
time: 44.7 us; the launch traced here: 44 us
  Pallas kernels  43.9 us (98%)
    pallas_call x1, Pallas kernels, far_field(): pl.pallas_call(functools.partial(far_kernel, gy_count), out_shape=(jax.Sh...  36.1 us
    pallas_call x1, Pallas kernels, near_field(): pl.pallas_call(near_kernel, out_shape=jax.ShapeDtypeStruct((PROBES, WIDTH...  7.78 us

profile of v6, /device:TPU:6, one launch (start us, length us, event | category | flops | bytes accessed | tf_op | source)
XLA Modules:
  0.0 44.0 jit_solution(18097047953418096141)
XLA Ops:
  0.0 36.1 %shard_map.136 = (f32[16,4096]{1,0:T(8,128)S(1)}, s32[8,128]{1,0:T(8,128)S(1)}, bf16[8,16,512]{2,1,0:T(8,128)(2,1)S(1)}, bf16[16,16,512]{2,1,0:T(8,128)(2,1)S(1)...) custom-call(bf16[3,4096]{1,0:T(4,128)(2,1)} %coords_hbm.1, ...), custom_call_target="tpu_custom_call" | custom-call | tf_op jit(solution)/shard_map/pallas_call | solution.py:407
  36.1 7.8 %shard_map.137 = f32[16,4096]{1,0:T(8,128)} custom-call(s32[8,128]{1,0:T(8,128)S(1)} %get-tuple-element.12.pairs_hbm, f32[16,4096]{1,0:T(8,128)S(1)} %get-tuple-element.13.total, bf16[8,16,512]{2,1,0:T(8,128)(2,1)S(1)} %get-tuple-element.14.own_vec, bf16[16,16,512]{2,1,0:T(8,128)(2,1)S(1)} %get-tuple-element.15.side_vec, ...), custom_call_target="tpu_custom_call" | custom-call | tf_op jit(solution)/shard_map/pallas_call | solution.py:507
